TPU v7x, 128 devices: a whole 4x4x4 slice. The times are simulated.
128 devices in a mesh: replica: 16 (over z_hi, x, core), fsdp: 8 (over y, z_lo).
Axes of the slice: x: 4, y: 4, z: 4 (z_hi: 2, z_lo: 2; z = z_hi * 2 + z_lo), core: 2. Of those that a mesh axis runs over, the one named last changes fastest.
Arguments:
- tokens: bfloat16 [16, 4096, 8192], P('replica', 'fsdp'), may hold values from -6 to 6
- targets: bfloat16 [16, 4096, 512], P('replica', 'fsdp'), may hold values from -6 to 6
- global_params: float32 [8192, 512], P('fsdp'), may hold values from -0.0625 to 0.0625
- drift: float32 [16, 8192, 512], P('replica', 'fsdp'), may hold values from -0.024 to 0.024
- first_moment: float32 [16, 8192, 512], P('replica', 'fsdp'), may hold values from -0.06 to 0.06
- second_moment: float32 [16, 8192, 512], P('replica', 'fsdp'), may hold values from 1e-05 to 0.001
- outer_momentum: float32 [8192, 512], P('fsdp'), may hold values from -0.03 to 0.03
Outputs:
- new_global: float32 [8192, 512], P('fsdp')
- new_momentum: float32 [8192, 512], P('fsdp')
All inputs are finite; a program needn't handle non-finite values.
Results may differ from a plain program's by a relative error of at most 0.00049.
Values may be sent and summed in bfloat16 or wider, within the bound.
A program may use at most 128 MiB of HBM per device.

v0:
```python
import jax
import jax.numpy as jnp
from jax import lax
from jax.sharding import PartitionSpec as P

corr_one = 1.0 - 0.9**20
corr_two = 1.0 - 0.95**20


def outer_step(global_rows, momentum_rows, average):
    momentum_next = 0.9 * momentum_rows + average
    global_next = global_rows - 0.7 * (0.9 * momentum_next + average)
    return (global_next, momentum_next)


def shards(tokens, targets, global_params, drift, first_moment, second_moment, outer_momentum):
    inputs = tokens[0]
    wanted = targets[0]
    local = global_params + drift[0]
    weight = local.astype(jnp.bfloat16)
    columns = inputs
    keys = jnp.dot(
        columns,
        lax.all_gather(weight, "fsdp", axis=0, tiled=True),
        preferred_element_type=jnp.float32,
    )
    resid = (keys - wanted.astype(jnp.float32)).astype(jnp.bfloat16)
    columns = inputs
    summed_grad = lax.psum_scatter(
        lax.dot_general(
            columns, resid, (((0,), (0,)), ((), ())), preferred_element_type=jnp.float32
        ),
        "fsdp",
        scatter_dimension=0,
        tiled=True,
    )
    grad = summed_grad / (inputs.shape[0] * lax.axis_size("fsdp"))
    moment = 0.9 * first_moment[0] + 0.1 * grad
    second = 0.95 * second_moment[0] + 0.05 * grad * grad
    update = moment / corr_one / (jnp.sqrt(second / corr_two) + 1e-08) + 0.1 * local
    local_new = local - 0.003 * update
    delta_wide = global_params - local_new
    replicas = lax.axis_size("replica")
    summed = lax.psum(delta_wide, "replica")
    new_global, new_momentum = outer_step(global_params, outer_momentum, summed / replicas)
    return (new_global, new_momentum)


def solution(mesh):
    in_specs = (
        P("replica", "fsdp", None),
        P("replica", "fsdp", None),
        P("fsdp", None),
        P("replica", "fsdp", None),
        P("replica", "fsdp", None),
        P("replica", "fsdp", None),
        P("fsdp", None),
    )
    out_specs = (P("fsdp", None), P("fsdp", None))
    return jax.shard_map(shards, mesh=mesh, in_specs=in_specs, out_specs=out_specs, check_vma=False)
```

profile of v0, /device:TPU:1, one launch (start us, length us, event | category | flops | bytes accessed | tf_op | source)
XLA Modules:
  0.0 708.7 jit_solution(673052394538184530)
XLA Ops:
  7.2 0.0 all-gather.2.cloned.1.call-start
  7.2 1.9 copy.15
  9.1 2.9 copy.10
  12.0 0.0 copy-start.1
  12.0 2.9 fusion.12
  15.0 0.0 all-gather.2.cloned.1.call-update
  15.0 0.0 reduce-scatter.2.cloned.1.call-start
  15.0 171.7 %all-gather.2.cloned.1.call-done = bf16[8192,512]{0,1:T(8,128)(2,1)} async-done(((bf16[1024,512]{0,1:T(8,128)(2,1)}), bf16[8192,512]{0,1:T(8,128)(2,1)}) %all-gather.2.cloned.1.call-update) | async-done | bytes 8388624 | tf_op jit(solution)/shard_map/all_gather | solution.py:24
  186.8 0.0 copy-done.1
  186.8 10.3 %fusion.19 = bf16[512,512]{1,0:T(8,128)(2,1)S(1)} fusion(bf16[8192,512]{0,1:T(8,128)(2,1)} %all-gather.2.cloned.1.call-done, bf16[1,512,8192]{2,1,0:T(8,128)(2,1)} %param.7, bf16[1,512,512]{2,1,0:T(8,128)(2,1)S(1)} %copy-done.1), kind=kOutput, calls=%fused_computation.21 | convolution fusion | flops 4295753728 | bytes 17825792 | tf_op jit(solution)/shard_map/dot_general | solution.py:22
  197.1 11.5 %convolution_bitcast_fusion = f32[8192,512]{0,1:T(8,128)} fusion(bf16[512,512]{1,0:T(8,128)(2,1)S(1)} %fusion.19, bf16[1,512,8192]{2,1,0:T(8,128)(2,1)} %param.7), kind=kOutput, calls=%fused_computation | convolution fusion | flops 4294967296 | bytes 25690112 | tf_op jit(solution)/shard_map/dot_general | solution.py:30
  208.6 0.0 reduce-scatter.2.cloned.1.call-update
  208.6 0.0 all-reduce.2.cloned.1.call-start
  208.7 2.9 copy.12
  211.6 2.9 copy.13
  214.4 326.2 %reduce-scatter.2.cloned.1.call-done = f32[1024,512]{0,1:T(8,128)} async-done(((f32[8192,512]{0,1:T(8,128)}), f32[1024,512]{0,1:T(8,128)}) %reduce-scatter.2.cloned.1.call-update) | async-done | bytes 2097168 | tf_op jit(solution)/shard_map/reduce_scatter | solution.py:29
  540.7 6.6 fusion.10
  547.2 0.0 all-reduce.2.cloned.1.call-update
  547.2 2.9 copy.9
  550.1 141.7 %all-reduce.2.cloned.1.call-done = f32[1024,512]{0,1:T(8,128)} async-done(((f32[1024,512]{0,1:T(8,128)}), f32[1024,512]{0,1:T(8,128)}) %all-reduce.2.cloned.1.call-update) | async-done | bytes 2097168 | tf_op jit(solution)/shard_map/psum | solution.py:44
  691.9 5.4 multiply_add_fusion
  697.3 0.0 copy-start
  697.3 3.0 copy.16
  700.3 0.0 copy-done
  700.3 1.8 copy.17
Async XLA Ops:
  7.2 179.6 %all-gather.2.cloned.1.call-start = ((), (), s32[]{:S(2)}) async-start(), calls=%async_computation.1 | async-start | bytes 9437184 | tf_op jit(solution)/shard_map/all_gather | solution.py:24
  12.0 174.7 %copy-start.1 = (bf16[1,512,512]{2,1,0:T(8,128)(2,1)S(1)}, bf16[1,512,512]{2,1,0:T(8,128)(2,1)}, u32[]{:S(2)}) copy-start(bf16[1,512,512]{2,1,0:T(8,128)(2,1)} %param.8) | copy-start | bytes 1572868
  15.0 525.7 %reduce-scatter.2.cloned.1.call-start = ((), (), s32[]{:S(2)}) async-start(), calls=%async_computation.2 | async-start | bytes 18874368 | tf_op jit(solution)/shard_map/reduce_scatter | solution.py:29
  208.6 483.3 %all-reduce.2.cloned.1.call-start = ((), (), s32[]{:S(2)}) async-start(), calls=%async_computation.3 | async-start | bytes 4194304 | tf_op jit(solution)/shard_map/psum | solution.py:44
  697.3 3.0 copy-start
Sparse Core Ops, SparseCore 0:
  15.1 171.6 all-gather.1
  208.7 331.8 reduce-scatter.1
  547.4 144.4 all-reduce.1
where the time goes:
time: 709 us
  waiting for transfers between devices  640 us (90%)
  matrix products  21.8 us (3%)
  local copies, waits for them, and re-layouts  18.3 us (3%)
  other arithmetic  14.9 us (2%)
  between operations  13.8 us (2%)
    reduce_scatter x1, waiting for transfers between devices, shards(): lax.psum_scatter(lax.dot_general(columns, resid, (((0,), (0,)), ((), ()))...  326 us
    all_gather x1, waiting for transfers between devices, shards(): lax.all_gather(weight, 'fsdp', axis=0, tiled=True)  172 us
    psum x1, waiting for transfers between devices, shards(): summed = lax.psum(delta_wide, 'replica')  142 us
    unnamed x11, local copies, waits for them, and re-layouts  18.3 us
  transfers between devices with their start and end apart: 3, of which 3 were waited for; matrix products, arithmetic and copies ran while one was open for 1% of the time, Pallas kernels for 0%

commit v1 on v0

v1 whole, which is shorter than its diff:
```python
import functools
import jax
import jax.numpy as jnp
from jax import lax
from jax.experimental import pallas as pl
from jax.experimental.pallas import tpu as pltpu
from jax.sharding import PartitionSpec as P

MESH = pl.DeviceIdType.MESH
F32 = jnp.float32
BF16 = jnp.bfloat16

corr_one = 1.0 - 0.9**20
corr_two = 1.0 - 0.95**20

TOK = 512
D = 8192
KV = 512
NS = 8
ROWS = D // NS
H = KV // 2
C = 4
R = ROWS // C
AP = (144, 112)
GP = (160, 96)
XR = R // 4
REPLICAS = 16


class Links:
    def __init__(self, send_sems, recv_sems):
        self.send_sems, self.recv_sems = send_sems, recv_sems
        self.index, self.sent = {}, []

    def _sems(self, name):
        i = self.index.setdefault(name, len(self.index))
        return self.send_sems.at[i], self.recv_sems.at[i]

    def send(self, name, src, dst, target):
        s, r = self._sems(name)
        copy = pltpu.make_async_remote_copy(
            src_ref=src, dst_ref=dst, send_sem=s, recv_sem=r, device_id=target, device_id_type=MESH
        )
        copy.start()
        self.sent.append(copy)

    def recv(self, name, dst, anyone):
        s, r = self._sems(name)
        pltpu.make_async_remote_copy(
            src_ref=dst, dst_ref=dst, send_sem=s, recv_sem=r, device_id=anyone, device_id_type=MESH
        ).wait_recv()

    def drain(self):
        for copy in self.sent:
            copy.wait_send()


N_MESSAGES = 192


def kernel(
    tok_hbm, tgt_hbm, gp_hbm, dr_hbm, m_hbm, v_hbm, out_hbm,
    tok, tokt, w, g, tgt, keys, resid, gp, dr, mo, ve,
    r_b1, r_b2, r_b3, r_b4, r_d1, r_d2, delta, r_c, r_x, r_z, avg,
    load_sem, part_sem, out_sem, send_sems, recv_sems,
):
    rep = lax.axis_index("replica")
    me = lax.axis_index("fsdp")
    zh, x, c = rep // 8, (rep // 2) % 4, rep % 2
    y, zl = me // 2, me % 2
    yp, ym, y2 = (y + 1) % 4, (y + 3) % 4, (y + 2) % 4
    oz = 1 - zl

    def shard(a, b):
        return a * 2 + b

    to_yp, to_ym = (rep, shard(yp, zl)), (rep, shard(ym, zl))
    to_z = (rep, shard(y, oz))
    to_c = (zh * 8 + x * 2 + (1 - c), me)
    to_x = [(zh * 8 + ((x + k) % 4) * 2 + c, me) for k in range(4)]
    to_zh = ((1 - zh) * 8 + x * 2 + c, me)
    friends = [to_yp, to_ym, to_z, to_c, to_x[1], to_x[2], to_x[3], to_zh]
    links = Links(send_sems, recv_sems)
    ydirs = ((0, to_yp, ym, yp), (1, to_ym, yp, ym))

    parts = []
    for k in range(C):
        rows = pl.ds(k * R, R)
        a = pltpu.make_async_copy(gp_hbm.at[rows], gp.at[rows], part_sem.at[0, k])
        b = pltpu.make_async_copy(dr_hbm.at[0, rows], dr.at[rows], part_sem.at[1, k])
        a.start()
        b.start()
        parts.append((a, b))
    load_tok = pltpu.make_async_copy(tok_hbm.at[0], tok, load_sem.at[0])
    load_tgt = pltpu.make_async_copy(tgt_hbm.at[0], tgt, load_sem.at[1])
    load_m = pltpu.make_async_copy(m_hbm.at[0], mo, load_sem.at[2])
    load_v = pltpu.make_async_copy(v_hbm.at[0], ve, load_sem.at[3])
    for copy in (load_tok, load_tgt, load_m, load_v):
        copy.start()

    barrier = pltpu.get_barrier_semaphore()
    for friend in friends:
        pl.semaphore_signal(barrier, inc=1, device_id=friend, device_id_type=MESH)

    def weights(k):
        for copy in parts[k]:
            copy.wait()
        rows = pl.ds(k * R, R)
        for h in range(2):
            cols = pl.ds(h * H, H)
            w[me, h, rows] = (gp[rows, cols] + dr[rows, cols]).astype(BF16)

    weights(0)
    pl.semaphore_wait(barrier, len(friends))

    def rows_of(k, part, split):
        if part is None:
            return pl.ds(k * R, R)
        return pl.ds(k * R + (split[0] if part else 0), split[part])

    def wpiece(s, k, part=None, h=None):
        rows = rows_of(k, part, AP)
        return w.at[s, :, rows] if h is None else w.at[s, h, rows]

    def wsend(name, piece, target):
        links.send(name, piece, piece, target)

    for k in range(C):
        if k:
            weights(k)
        for h, target, _, _ in ydirs:
            wsend(("a1", h, k), wpiece(me, k), target)
        wsend(("za", k), wpiece(me, k), to_z)

    load_tok.wait()

    def dot_keys(s, k):
        cols = pl.ds(pl.multiple_of(s * ROWS + k * R, R), R)
        for h in range(2):
            keys[h] += jnp.dot(tok[:, cols], w[s, h, pl.ds(k * R, R)], preferred_element_type=F32)

    own_cols = pl.ds(pl.multiple_of(me * ROWS, ROWS), ROWS)
    for h in range(2):
        keys[h] = jnp.dot(tok[:, own_cols], w[me, h], preferred_element_type=F32)

    @pl.loop(0, D // 256)
    def _(b):
        at = pl.ds(pl.multiple_of(b * 256, 256), 256)
        tokt[at, :] = tok[:, at].T

    for k in range(C):
        links.recv(("za", k), wpiece(shard(y, oz), k), to_z)
        for h, target, _, _ in ydirs:
            wsend(("a2", h, k), wpiece(shard(y, oz), k, 0), target)
        for h, target, src, _ in ydirs:
            links.recv(("a1", h, k), wpiece(shard(src, zl), k), target)
            wsend(("a3", h, k), wpiece(shard(src, zl), k, None, h), target)
            wsend(("z3", h, k), wpiece(shard(src, zl), k, 1), to_z)
        dot_keys(shard(y, oz), k)
        dot_keys(shard(ym, zl), k)
        dot_keys(shard(yp, zl), k)
    for k in range(C):
        for h, target, src, _ in ydirs:
            links.recv(("a3", h, k), wpiece(shard(y2, zl), k, None, h), target)
            wsend(("z5", h, k), wpiece(shard(y2, zl), k, 1, h), to_z)
        for h, target, src, _ in ydirs:
            links.recv(("a2", h, k), wpiece(shard(src, oz), k, 0), target)
            wsend(("a4", h, k), wpiece(shard(src, oz), k, 0, h), target)
        dot_keys(shard(y2, zl), k)
    for k in range(C):
        for h, target, src, _ in ydirs:
            links.recv(("z3", h, k), wpiece(shard(src, oz), k, 1), to_z)
            dot_keys(shard(src, oz), k)
        for h, target, src, _ in ydirs:
            links.recv(("z5", h, k), wpiece(shard(y2, oz), k, 1, h), to_z)
            links.recv(("a4", h, k), wpiece(shard(y2, oz), k, 0, h), target)
        dot_keys(shard(y2, oz), k)

    load_tgt.wait()
    for h in range(2):
        resid[h] = (keys[h] - tgt[:, pl.ds(h * H, H)].astype(F32)).astype(BF16)

    def grads(s, k):
        at = pl.ds(pl.multiple_of(s * ROWS + k * R, R), R)
        for h in range(2):
            g[s, h, pl.ds(k * R, R)] = jnp.dot(
                tokt[at, :], resid[h], preferred_element_type=F32
            ).astype(BF16)

    def gpiece(s, k, part, h=None):
        rows = rows_of(k, part, GP)
        return g.at[s, :, rows] if h is None else g.at[s, h, rows]

    def part_rows(k, part):
        return pl.ds(k * GP[part], GP[part])

    def s1(k):
        for z in range(2):
            grads(shard(y2, z), k)
        for h, target, _, _ in ydirs:
            for z in range(2):
                links.send(
                    ("b1", h, z, k), gpiece(shard(y2, z), k, 0, h), r_b1.at[h, z, part_rows(k, 0)], target
                )
        links.send(("d1", 2, k), gpiece(shard(y2, oz), k, 1), r_d1.at[2, :, part_rows(k, 1)], to_z)

        @pl.loop(0, 2)
        def _(z):
            for a in (yp, ym, y):
                grads(shard(a, z), k)

        for j, a in ((1, yp), (3, ym), (0, y)):
            links.send(("d1", j, k), gpiece(shard(a, oz), k, 1), r_d1.at[j, :, part_rows(k, 1)], to_z)

    def s2y(k):
        p = part_rows(k, 0)
        for h, target, _, dst in ydirs:
            for z in range(2):
                links.recv(("b1", h, z, k), r_b1.at[h, z, p], target)
                own = gpiece(shard(dst, z), k, 0, h)
                own[...] += r_b1[h, z, p]
                links.send(("b2", h, z, k), gpiece(shard(dst, z), k, 0), r_b2.at[h, z, :, p], target)

    def s2z(k):
        p = part_rows(k, 1)
        links.recv(("d1", 2, k), r_d1.at[2, :, p], to_z)
        own = gpiece(shard(y2, zl), k, 1)
        own[...] += r_d1[2, :, p]
        for h, target, _, _ in ydirs:
            links.send(("b3", h, k), gpiece(shard(y2, zl), k, 1, h), r_b3.at[h, p], target)

    def s3y(k):
        p = part_rows(k, 1)
        for h, target, _, dst in ydirs:
            j = 1 if h == 0 else 3
            links.recv(("d1", j, k), r_d1.at[j, :, p], to_z)
            links.recv(("b3", h, k), r_b3.at[h, p], target)
            one = gpiece(shard(dst, zl), k, 1, h)
            one[...] += r_d1[j, h, p] + r_b3[h, p]
            two = gpiece(shard(dst, zl), k, 1, 1 - h)
            two[...] += r_d1[j, 1 - h, p]
            links.send(("b4", h, k), gpiece(shard(dst, zl), k, 1), r_b4.at[h, :, p], target)

    def s3z(k):
        p = part_rows(k, 0)
        for h, target, _, _ in ydirs:
            for z in range(2):
                links.recv(("b2", h, z, k), r_b2.at[h, z, :, p], target)
        own = gpiece(shard(y, oz), k, 0)
        own[...] += r_b2[0, oz, :, p] + r_b2[1, oz, :, p]
        links.send(("d2", k), own, r_d2.at[:, p], to_z)

    def update(rows, cols, grad_sum):
        grad = grad_sum * (1.0 / (TOK * NS))
        glob = gp[rows, cols]
        local = glob + dr[rows, cols]
        moment = 0.9 * mo[rows, cols] + 0.1 * grad
        second = 0.95 * ve[rows, cols] + 0.05 * grad * grad
        step = moment / corr_one / (jnp.sqrt(second / corr_two) + 1e-08) + 0.1 * local
        return glob - (local - 0.003 * step)

    def s4(k):
        if k == 0:
            load_m.wait()
            load_v.wait()
        links.recv(("d2", k), r_d2.at[:, part_rows(k, 0)], to_z)
        sub = 32

        @pl.loop(0, GP[0] // sub)
        def _(i):
            off = pl.multiple_of(i * sub, sub)
            rows = pl.ds(k * R + off, sub)
            p = pl.ds(k * GP[0] + off, sub)
            for h in range(2):
                total = (
                    (g[me, h, rows].astype(F32) + r_d2[h, p].astype(F32))
                    + (r_b2[0, zl, h, p].astype(F32) + r_b2[1, zl, h, p].astype(F32))
                )
                delta[h, rows] = update(rows, pl.ds(h * H, H), total)

        links.recv(("d1", 0, k), r_d1.at[0, :, part_rows(k, 1)], to_z)
        for h, target, _, _ in ydirs:
            links.recv(("b4", h, k), r_b4.at[h, :, part_rows(k, 1)], target)

        @pl.loop(0, GP[1] // sub)
        def _(i):
            off = pl.multiple_of(i * sub, sub)
            rows = pl.ds(k * R + GP[0] + off, sub)
            p = pl.ds(k * GP[1] + off, sub)
            for h in range(2):
                total = (
                    (g[me, h, rows].astype(F32) + r_d1[0, h, p].astype(F32))
                    + (r_b4[0, h, p].astype(F32) + r_b4[1, h, p].astype(F32))
                )
                delta[h, rows] = update(rows, pl.ds(h * H, H), total)

        rows = pl.ds(k * R, R)
        links.send(("c", k), delta.at[1 - c, rows], r_c.at[rows], to_c)

    def x_rows(k, a):
        return pl.ds(pl.multiple_of(k * R + a * XR, XR), XR)

    def s5(k):
        rows = pl.ds(k * R, R)
        links.recv(("c", k), r_c.at[rows], to_c)
        delta[c, rows] += r_c[rows]
        for j in (2, 1, 3):
            links.send(
                ("x", j, k), delta.at[c, x_rows(k, (x + j) % 4)], r_x.at[j - 1, pl.ds(k * XR, XR)], to_x[j]
            )

    def s6(k):
        p = pl.ds(k * XR, XR)
        for j in (1, 3, 2):
            links.recv(("x", j, k), r_x.at[j - 1, p], to_x[j])
        at = x_rows(k, x)
        delta[c, at] += r_x[0, p] + r_x[1, p] + r_x[2, p]
        links.send(("zh", k), delta.at[c, at], r_z.at[p], to_zh)

    def s7(k):
        p = pl.ds(k * XR, XR)
        links.recv(("zh", k), r_z.at[p], to_zh)
        at = x_rows(k, x)
        avg[c, at] = (delta[c, at] + r_z[p]) * (1.0 / REPLICAS)
        for j in (2, 1, 3):
            links.send(("xg", j, k), avg.at[c, at], avg.at[c, at], to_x[j])

    out_copies = []

    def write_out(h, k):
        rows = pl.ds(k * R, R)
        cols = pl.ds(pl.multiple_of(h * H, H), H)
        copy = pltpu.make_async_copy(avg.at[h, rows], out_hbm.at[rows, cols], out_sem.at[len(out_copies)])
        copy.start()
        out_copies.append(copy)

    def s8(k):
        for j in (1, 3, 2):
            links.recv(("xg", j, k), avg.at[c, x_rows(k, (x + 4 - j) % 4)], to_x[j])
        rows = pl.ds(k * R, R)
        links.send(("cg", k), avg.at[c, rows], avg.at[c, rows], to_c)
        write_out(c, k)

    def s9(k):
        rows = pl.ds(k * R, R)
        links.recv(("cg", k), avg.at[1 - c, rows], to_c)
        write_out(1 - c, k)

    order = [
        (s1, 0), (s1, 1), (s2y, 0), (s2z, 0), (s1, 2), (s2y, 1), (s3z, 0), (s3y, 0), (s2z, 1), (s1, 3),
        (s2y, 2), (s4, 0), (s3z, 1), (s3y, 1), (s5, 0), (s2z, 2), (s2y, 3), (s6, 0), (s2z, 3), (s4, 1),
        (s7, 0), (s3z, 2), (s5, 1), (s3y, 2), (s8, 0), (s6, 1), (s3z, 3), (s3y, 3), (s4, 2), (s7, 1), (s9, 0), (s5, 2),
        (s8, 1), (s4, 3), (s6, 2), (s5, 3), (s7, 2), (s6, 3), (s9, 1), (s7, 3), (s8, 2), (s8, 3), (s9, 2), (s9, 3),
    ]
    for stage, k in order:
        stage(k)

    for copy in out_copies:
        copy.wait()
    links.drain()


def replica_average(tokens, targets, global_params, drift, first_moment, second_moment):
    any_space = pl.BlockSpec(memory_space=pl.ANY)
    p1, p2 = C * GP[0], C * GP[1]
    return pl.pallas_call(
        kernel,
        out_shape=jax.ShapeDtypeStruct((ROWS, KV), F32),
        in_specs=[any_space] * 6,
        out_specs=any_space,
        scratch_shapes=[
            pltpu.VMEM((TOK, D), BF16),
            pltpu.VMEM((D, TOK), BF16),
            pltpu.VMEM((NS, 2, ROWS, H), BF16),
            pltpu.VMEM((NS, 2, ROWS, H), BF16),
            pltpu.VMEM((TOK, KV), BF16),
            pltpu.VMEM((2, TOK, H), F32),
            pltpu.VMEM((2, TOK, H), BF16),
            pltpu.VMEM((ROWS, KV), F32),
            pltpu.VMEM((ROWS, KV), F32),
            pltpu.VMEM((ROWS, KV), F32),
            pltpu.VMEM((ROWS, KV), F32),
            pltpu.VMEM((2, 2, p1, H), BF16),
            pltpu.VMEM((2, 2, 2, p1, H), BF16),
            pltpu.VMEM((2, p2, H), BF16),
            pltpu.VMEM((2, 2, p2, H), BF16),
            pltpu.VMEM((4, 2, p2, H), BF16),
            pltpu.VMEM((2, p1, H), BF16),
            pltpu.VMEM((2, ROWS, H), F32),
            pltpu.VMEM((ROWS, H), F32),
            pltpu.VMEM((3, C * XR, H), F32),
            pltpu.VMEM((C * XR, H), F32),
            pltpu.VMEM((2, ROWS, H), F32),
            pltpu.SemaphoreType.DMA((4,)),
            pltpu.SemaphoreType.DMA((2, C)),
            pltpu.SemaphoreType.DMA((2 * C,)),
            pltpu.SemaphoreType.DMA((N_MESSAGES,)),
            pltpu.SemaphoreType.DMA((N_MESSAGES,)),
        ],
        compiler_params=pltpu.CompilerParams(
            collective_id=0, has_side_effects=True, vmem_limit_bytes=62 * 2**20
        ),
        cost_estimate=pl.CostEstimate(
            flops=4 * TOK * D * KV, bytes_accessed=24 * 2**20, transcendentals=ROWS * KV
        ),
        name="inner_step_and_average",
    )(tokens, targets, global_params, drift, first_moment, second_moment)


def shards(tokens, targets, global_params, drift, first_moment, second_moment, outer_momentum):
    average = replica_average(tokens, targets, global_params, drift, first_moment, second_moment)
    momentum_next = 0.9 * outer_momentum + average
    global_next = global_params - 0.7 * (0.9 * momentum_next + average)
    return (global_next, momentum_next)


def solution(mesh):
    in_specs = (
        P("replica", "fsdp", None),
        P("replica", "fsdp", None),
        P("fsdp", None),
        P("replica", "fsdp", None),
        P("replica", "fsdp", None),
        P("replica", "fsdp", None),
        P("fsdp", None),
    )
    out_specs = (P("fsdp", None), P("fsdp", None))
    return jax.shard_map(shards, mesh=mesh, in_specs=in_specs, out_specs=out_specs, check_vma=False)
```

time: 709 us -> 153 us (0.22)
  waiting for transfers between devices: 640 us -> 0 us
  Pallas kernels: 0 us -> 146 us
  matrix products: 21.8 us -> 0 us
  local copies, waits for them, and re-layouts: 18.3 us -> 0 us
  between operations: 13.8 us -> 0.64 us
  other arithmetic: 14.9 us -> 5.65 us
    reduce_scatter x1 -> x0, waiting for transfers between devices: 326 us -> none  [shards(): lax.psum_scatter(lax.dot_general(columns, resid, (((0,), (0,)), ((), ()))...]
    all_gather x1 -> x0, waiting for transfers between devices: 172 us -> none  [shards(): lax.all_gather(weight, 'fsdp', axis=0, tiled=True)]
    pallas_call x0 -> x1, Pallas kernels: none -> 146 us  [replica_average(): pl.pallas_call(kernel, out_shape=jax.ShapeDtypeStruct((ROWS, KV), F32), i...]
    psum x1 -> x0, waiting for transfers between devices: 142 us -> none  [shards(): summed = lax.psum(delta_wide, 'replica')]
    dot_general x2 -> x0, matrix products: 21.8 us -> none  [the longest x1 11.5 us: shards(): lax.dot_general(columns, resid, (((0,), (0,)), ((), ())), preferred_eleme...]
    unnamed x11 -> x0, local copies, waits for them, and re-layouts: 18.3 us -> none
  transfers between devices with their start and end apart: 3 -> 0, of which waited for: 3 -> 0; matrix products, arithmetic and copies ran while one was open for 1% -> 0% of each run, Pallas kernels for 0% -> 0%
where the time goes in v1:
time: 153 us
  Pallas kernels  146 us (95%)
  other arithmetic  5.65 us (4%)
    pallas_call x1, Pallas kernels, replica_average(): pl.pallas_call(kernel, out_shape=jax.ShapeDtypeStruct((ROWS, KV), F32), i...  146 us
    sub x1, other arithmetic, shards(): global_next = global_params - 0.7 * (0.9 * momentum_next + average)  5.65 us

profile of v1, /device:TPU:1, one launch (start us, length us, event | category | flops | bytes accessed | tf_op | source)
XLA Modules:
  0.0 152.7 jit_solution(14132122486471997158)
XLA Ops:
  0.6 146.4 %inner_step_and_average.1 = f32[1024,512]{1,0:T(8,128)} custom-call(bf16[1,512,8192]{2,1,0:T(8,128)(2,1)} %tok_hbm.1, bf16[1,512,512]{2,1,0:T(8,128)(2,1)} %tgt_hbm.1, f32[1024,512]{1,0:T(8,128)} %gp_hbm.1, f32[1,1024,512]{2,1,0:T(8,128)} %dr_hbm.1, f32[1,1024,512]{2,1,0:T(8,128)} %m_hbm.1, f32[1,1024,512]{2,1,0:T(8,128)} %v_hbm.1), custom_call_target="tpu_custom_call" | custom-call | flops 8589934592 | bytes 25165824 | tf_op jit(solution)/shard_map/inner_step_and_average/pallas_call | solution.py:366
  147.0 5.7 %multiply_subtract_fusion = (f32[1024,512]{1,0:T(8,128)}, f32[1024,512]{1,0:T(8,128)}) fusion(f32[1024,512]{1,0:T(8,128)} %gp_hbm.1, f32[1024,512]{1,0:T(8,128)} %inner_step_and_average.1, f32[1024,512]{1,0:T(8,128)} %param.13), kind=kLoop, calls=%fused_computation | loop fusion | flops 3145728 | bytes 10485760 | tf_op jit(solution)/shard_map/sub | solution.py:413

commit v2 on v1

v2 whole, which is shorter than its diff:
```python
import functools
import jax
import jax.numpy as jnp
from jax import lax
from jax.experimental import pallas as pl
from jax.experimental.pallas import tpu as pltpu
from jax.sharding import PartitionSpec as P

MESH = pl.DeviceIdType.MESH
F32 = jnp.float32
BF16 = jnp.bfloat16

corr_one = 1.0 - 0.9**20
corr_two = 1.0 - 0.95**20

TOK = 512
D = 8192
KV = 512
NS = 8
ROWS = D // NS
H = KV // 2
C = 4
R = ROWS // C
AP = (144, 112)
GROUPS = ((144, 112), (160, 96), (144, 112), (64, 64), (48, 16), (32, 32))
N = len(GROUPS)
FAST = 1
SIZE = [sum(p) for p in GROUPS]
START = [sum(SIZE[:k]) for k in range(N)]
PSTART = [[sum(p[i] for p in GROUPS[:k]) for k in range(N)] for i in range(2)]
PROWS = [sum(p[i] for p in GROUPS) for i in range(2)]
REPLICAS = 16
VMEM_KIB = 50176


class Links:
    def __init__(self, send_sems, recv_sems):
        self.send_sems, self.recv_sems = send_sems, recv_sems
        self.index, self.sent = {}, []

    def _sems(self, name):
        i = self.index.setdefault(name, len(self.index))
        return self.send_sems.at[i], self.recv_sems.at[i]

    def send(self, name, src, dst, target):
        s, r = self._sems(name)
        copy = pltpu.make_async_remote_copy(
            src_ref=src, dst_ref=dst, send_sem=s, recv_sem=r, device_id=target, device_id_type=MESH
        )
        copy.start()
        self.sent.append(copy)

    def recv(self, name, dst, anyone):
        s, r = self._sems(name)
        pltpu.make_async_remote_copy(
            src_ref=dst, dst_ref=dst, send_sem=s, recv_sem=r, device_id=anyone, device_id_type=MESH
        ).wait_recv()

    def drain(self):
        for copy in self.sent:
            copy.wait_send()
        self.sent = []


N_MESSAGES = 208


def kernel(
    tok_hbm, tgt_hbm, gp_hbm, dr_hbm, m_hbm, v_hbm, om_hbm, new_global, new_momentum,
    tok, tokt, w, tgt, gp, dr, mo, ve, om,
    r_b1, r_b2, r_b3, r_b4, r_d1, r_d2, delta, r_c, r_x, r_z, r_f, avg,
    load_sem, part_sem, send_sems, recv_sems,
):
    rep = lax.axis_index("replica")
    me = lax.axis_index("fsdp")
    zh, x, c = rep // 8, (rep // 2) % 4, rep % 2
    y, zl = me // 2, me % 2
    yp, ym, y2 = (y + 1) % 4, (y + 3) % 4, (y + 2) % 4
    oz = 1 - zl

    def shard(a, b):
        return a * 2 + b

    to_yp, to_ym = (rep, shard(yp, zl)), (rep, shard(ym, zl))
    to_z = (rep, shard(y, oz))
    to_x = [(zh * 8 + ((x + k) % 4) * 2 + c, me) for k in range(4)]
    to_zh = ((1 - zh) * 8 + x * 2 + c, me)
    to_xc = [(zh * 8 + ((x + k) % 4) * 2 + (1 - c), me) for k in range(4)]
    friends = [to_yp, to_ym, to_z, to_zh] + to_x[1:] + to_xc
    links = Links(send_sems, recv_sems)
    ydirs = ((0, to_yp, ym, yp), (1, to_ym, yp, ym))

    parts = []
    for k in range(C):
        rows = pl.ds(k * R, R)
        a = pltpu.make_async_copy(gp_hbm.at[rows], gp.at[rows], part_sem.at[0, k])
        b = pltpu.make_async_copy(dr_hbm.at[0, rows], dr.at[rows], part_sem.at[1, k])
        a.start()
        b.start()
        parts.append((a, b))
    load_tok = pltpu.make_async_copy(tok_hbm.at[0], tok, load_sem.at[0])
    load_tgt = pltpu.make_async_copy(tgt_hbm.at[0], tgt, load_sem.at[1])
    load_m = pltpu.make_async_copy(m_hbm.at[0], mo, load_sem.at[2])
    load_v = pltpu.make_async_copy(v_hbm.at[0], ve, load_sem.at[3])
    load_om = pltpu.make_async_copy(om_hbm, om, load_sem.at[4])
    for copy in (load_tok, load_tgt, load_m, load_v, load_om):
        copy.start()

    barrier = pltpu.get_barrier_semaphore()
    for friend in friends:
        pl.semaphore_signal(barrier, inc=1, device_id=friend, device_id_type=MESH)

    def weights(k):
        for copy in parts[k]:
            copy.wait()
        rows = pl.ds(k * R, R)
        for h in range(2):
            cols = pl.ds(h * H, H)
            w[me, h, rows] = (gp[rows, cols] + dr[rows, cols]).astype(BF16)

    weights(0)
    pl.semaphore_wait(barrier, len(friends))

    def wpiece(s, k, part=None, h=None):
        rows = pl.ds(k * R, R) if part is None else pl.ds(k * R + (AP[0] if part else 0), AP[part])
        return w.at[s, :, rows] if h is None else w.at[s, h, rows]

    def wsend(name, piece, target):
        links.send(name, piece, piece, target)

    for k in range(C):
        if k:
            weights(k)
        for h, target, _, _ in ydirs:
            wsend(("a1", h, k), wpiece(me, k), target)
        wsend(("za", k), wpiece(me, k), to_z)

    load_tok.wait()
    keys = delta.at[:, pl.ds(0, TOK)]

    def dot_keys(s, k):
        cols = pl.ds(pl.multiple_of(s * ROWS + k * R, R), R)
        for h in range(2):
            keys[h] += jnp.dot(tok[:, cols], w[s, h, pl.ds(k * R, R)], preferred_element_type=F32)

    own_cols = pl.ds(pl.multiple_of(me * ROWS, ROWS), ROWS)
    for h in range(2):
        keys[h] = jnp.dot(tok[:, own_cols], w[me, h], preferred_element_type=F32)

    @pl.loop(0, D // 256)
    def _(b):
        at = pl.ds(pl.multiple_of(b * 256, 256), 256)
        tokt[at, :] = tok[:, at].T

    for k in range(C):
        links.recv(("za", k), wpiece(shard(y, oz), k), to_z)
        for h, target, _, _ in ydirs:
            wsend(("a2", h, k), wpiece(shard(y, oz), k, 0), target)
        for h, target, src, _ in ydirs:
            links.recv(("a1", h, k), wpiece(shard(src, zl), k), target)
            wsend(("a3", h, k), wpiece(shard(src, zl), k, None, h), target)
            wsend(("z3", h, k), wpiece(shard(src, zl), k, 1), to_z)
        dot_keys(shard(y, oz), k)
        dot_keys(shard(ym, zl), k)
        dot_keys(shard(yp, zl), k)
    for k in range(C):
        for h, target, src, _ in ydirs:
            links.recv(("a3", h, k), wpiece(shard(y2, zl), k, None, h), target)
            wsend(("z5", h, k), wpiece(shard(y2, zl), k, 1, h), to_z)
        for h, target, src, _ in ydirs:
            links.recv(("a2", h, k), wpiece(shard(src, oz), k, 0), target)
            wsend(("a4", h, k), wpiece(shard(src, oz), k, 0, h), target)
        dot_keys(shard(y2, zl), k)
    for k in range(C):
        for h, target, src, _ in ydirs:
            links.recv(("z3", h, k), wpiece(shard(src, oz), k, 1), to_z)
            dot_keys(shard(src, oz), k)
        for h, target, src, _ in ydirs:
            links.recv(("z5", h, k), wpiece(shard(y2, oz), k, 1, h), to_z)
            links.recv(("a4", h, k), wpiece(shard(y2, oz), k, 0, h), target)
        dot_keys(shard(y2, oz), k)

    load_tgt.wait()
    for h in range(2):
        cols = pl.ds(h * H, H)
        tgt[:, cols] = (keys[h] - tgt[:, cols].astype(F32)).astype(BF16)

    links.drain()
    g = w

    def grads(s, k):
        at = pl.ds(pl.multiple_of(s * ROWS + START[k], 16), SIZE[k])
        for h in range(2):
            g[s, h, pl.ds(START[k], SIZE[k])] = jnp.dot(
                tokt[at, :], tgt[:, pl.ds(h * H, H)], preferred_element_type=F32
            ).astype(BF16)

    def grows(k, part):
        return pl.ds(START[k] + (GROUPS[k][0] if part else 0), GROUPS[k][part])

    def gpiece(s, k, part, h=None):
        return g.at[s, :, grows(k, part)] if h is None else g.at[s, h, grows(k, part)]

    def gpair(a, k, h=None):
        two = pl.ds(pl.multiple_of(a * 2, 2), 2)
        return g.at[two, :, grows(k, 0)] if h is None else g.at[two, h, grows(k, 0)]

    def part_rows(k, part):
        return pl.ds(PSTART[part][k], GROUPS[k][part])

    def s1a(k):
        for z in range(2):
            grads(shard(y2, z), k)
        for h, target, _, _ in ydirs:
            links.send(("b1", h, k), gpair(y2, k, h), r_b1.at[h, :, part_rows(k, 0)], target)
        links.send(("d1", 2, k), gpiece(shard(y2, oz), k, 1), r_d1.at[2, :, part_rows(k, 1)], to_z)

    def s1b(k):
        @pl.loop(0, 2)
        def _(z):
            for a in (yp, ym, y):
                grads(shard(a, z), k)

        for j, a in ((1, yp), (3, ym), (0, y)):
            links.send(("d1", j, k), gpiece(shard(a, oz), k, 1), r_d1.at[j, :, part_rows(k, 1)], to_z)

    def s2y(h, k):
        p = part_rows(k, 0)
        _, target, _, dst = ydirs[h]
        links.recv(("b1", h, k), r_b1.at[h, :, p], target)
        own = gpair(dst, k, h)
        own[...] += r_b1[h, :, p]
        links.send(("b2", h, k), gpair(dst, k), r_b2.at[h, :, :, p], target)

    def s2z(k):
        p = part_rows(k, 1)
        links.recv(("d1", 2, k), r_d1.at[2, :, p], to_z)
        own = gpiece(shard(y2, zl), k, 1)
        own[...] += r_d1[2, :, p]
        for h, target, _, _ in ydirs:
            links.send(("b3", h, k), gpiece(shard(y2, zl), k, 1, h), r_b3.at[h, p], target)

    def s3y(h, k):
        p = part_rows(k, 1)
        _, target, _, dst = ydirs[h]
        j = 1 if h == 0 else 3
        links.recv(("d1", j, k), r_d1.at[j, :, p], to_z)
        links.recv(("b3", h, k), r_b3.at[h, p], target)
        one = gpiece(shard(dst, zl), k, 1, h)
        one[...] += r_d1[j, h, p] + r_b3[h, p]
        two = gpiece(shard(dst, zl), k, 1, 1 - h)
        two[...] += r_d1[j, 1 - h, p]
        links.send(("b4", h, k), gpiece(shard(dst, zl), k, 1), r_b4.at[h, :, p], target)

    def s3z(k):
        p = part_rows(k, 0)
        for h, target, _, _ in ydirs:
            links.recv(("b2", h, k), r_b2.at[h, :, :, p], target)
        own = gpiece(shard(y, oz), k, 0)
        own[...] += r_b2[0, oz, :, p] + r_b2[1, oz, :, p]
        links.send(("d2", k), own, r_d2.at[:, p], to_z)

    def update(rows, cols, grad_sum):
        grad = grad_sum * (1.0 / (TOK * NS))
        glob = gp[rows, cols]
        local = glob + dr[rows, cols]
        moment = 0.9 * mo[rows, cols] + 0.1 * grad
        second = 0.95 * ve[rows, cols] + 0.05 * grad * grad
        step = moment / corr_one / (jnp.sqrt(second / corr_two) + 1e-08) + 0.1 * local
        return glob - (local - 0.003 * step)

    def updates(k, part, total):
        sub = next(b for b in (48, 32, 16) if GROUPS[k][part] % b == 0)

        @pl.loop(0, GROUPS[k][part] // sub)
        def _(i):
            off = pl.multiple_of(i * sub, 16)
            rows = pl.ds(START[k] + (GROUPS[k][0] if part else 0) + off, sub)
            p = pl.ds(PSTART[part][k] + off, sub)
            for h in range(2):
                delta[h, rows] = update(rows, pl.ds(h * H, H), total(h, rows, p))

    def s4(k):
        if k == 0:
            load_m.wait()
            load_v.wait()
        links.recv(("d2", k), r_d2.at[:, part_rows(k, 0)], to_z)
        updates(
            k, 0,
            lambda h, rows, p: (g[me, h, rows].astype(F32) + r_d2[h, p].astype(F32))
            + (r_b2[0, zl, h, p].astype(F32) + r_b2[1, zl, h, p].astype(F32)),
        )
        links.recv(("d1", 0, k), r_d1.at[0, :, part_rows(k, 1)], to_z)
        for h, target, _, _ in ydirs:
            links.recv(("b4", h, k), r_b4.at[h, :, part_rows(k, 1)], target)
        updates(
            k, 1,
            lambda h, rows, p: (g[me, h, rows].astype(F32) + r_d1[0, h, p].astype(F32))
            + (r_b4[0, h, p].astype(F32) + r_b4[1, h, p].astype(F32)),
        )
        if k < N - FAST:
            rows = pl.ds(START[k], SIZE[k])
            links.send(("c", k), delta.at[1 - c, rows], r_c.at[rows], to_xc[0])
        else:
            for j, other, target in others():
                half = 1 - c if other else c
                links.send(
                    ("x", j, other, k), delta.at[half, x_rows(k, (x + j) % 4)], f_slot(j, other, k), target
                )

    def others():
        found = [(j, 0, to_x[j]) for j in (2, 1, 3)] + [(j, 1, to_xc[j]) for j in (2, 1, 3, 0)]
        return sorted(found, key=lambda f: (2, 1, 3, 0).index(f[0]))

    def x_rows(k, a):
        q = SIZE[k] // 4
        return pl.ds(pl.multiple_of(START[k] + a * q, 8), q)

    def q_rows(k):
        return pl.ds(START[k] // 4, SIZE[k] // 4)

    def f_slot(j, other, k):
        q = SIZE[k] // 4
        return r_f.at[j * 2 + other, pl.ds((START[k] - START[N - FAST]) // 4, q)]

    def s5(k):
        rows = pl.ds(START[k], SIZE[k])
        links.recv(("c", k), r_c.at[rows], to_xc[0])
        delta[c, rows] += r_c[rows]
        for j in (2, 1, 3):
            links.send(
                ("x", j, k), delta.at[c, x_rows(k, (x + j) % 4)], r_x.at[j - 1, q_rows(k)], to_x[j]
            )

    def s6(k):
        at = x_rows(k, x)
        if k < N - FAST:
            p = q_rows(k)
            for j in (1, 3, 2):
                links.recv(("x", j, k), r_x.at[j - 1, p], to_x[j])
            delta[c, at] += r_x[0, p] + r_x[1, p] + r_x[2, p]
        else:
            for j, other, target in reversed(others()):
                links.recv(("x", j, other, k), f_slot(j, other, k), target)
            total = delta[c, at]
            for j, other, _ in others():
                total += f_slot(j, other, k)[...]
            delta[c, at] = total
        links.send(("zh", k), delta.at[c, at], r_z.at[q_rows(k)], to_zh)

    def s7(k):
        links.recv(("zh", k), r_z.at[q_rows(k)], to_zh)
        at = x_rows(k, x)
        avg[c, at] = (delta[c, at] + r_z[q_rows(k)]) * (1.0 / REPLICAS)
        if k < N - FAST:
            for j in (2, 1, 3):
                links.send(("xg", j, k), avg.at[c, at], avg.at[c, at], to_x[j])
        else:
            for j, other, target in others():
                links.send(("xg", j, other, k), avg.at[c, at], avg.at[c, at], target)

    def outer(k, half):
        sub = 32

        @pl.loop(0, SIZE[k] // sub)
        def _(i):
            rows = pl.ds(START[k] + pl.multiple_of(i * sub, sub), sub)
            cols = pl.ds(pl.multiple_of(half * H, H), H)
            average = avg[half, rows]
            momentum_next = 0.9 * om[rows, cols] + average
            new_momentum[rows, cols] = momentum_next
            new_global[rows, cols] = gp[rows, cols] - 0.7 * (0.9 * momentum_next + average)

    def s8(k):
        for j in (1, 3, 2):
            links.recv(("xg", j, k), avg.at[c, x_rows(k, (x + 4 - j) % 4)], to_x[j])
        rows = pl.ds(START[k], SIZE[k])
        links.send(("cg", k), avg.at[c, rows], avg.at[c, rows], to_xc[0])
        if k == 0:
            load_om.wait()
        outer(k, c)

    def s9(k):
        if k < N - FAST:
            rows = pl.ds(START[k], SIZE[k])
            links.recv(("cg", k), avg.at[1 - c, rows], to_xc[0])
            outer(k, 1 - c)
        else:
            for j, other, target in reversed(others()):
                half = 1 - c if other else c
                links.recv(("xg", j, other, k), avg.at[half, x_rows(k, (x + 4 - j) % 4)], target)
            outer(k, 0)
            outer(k, 1)

    s2y0, s2y1 = functools.partial(s2y, 0), functools.partial(s2y, 1)
    s3y0, s3y1 = functools.partial(s3y, 0), functools.partial(s3y, 1)
    order = (
        (s1a, 3), (s1a, 0), (s1b, 0), (s1a, 1), (s2y1, 0), (s2y0, 0), (s1b, 1), (s2y1, 1), (s2y0, 1), (s2z, 0),
        (s2z, 1), (s1a, 2), (s3z, 0), (s3y1, 0), (s3y0, 0), (s1b, 3), (s2z, 2), (s3z, 1), (s1b, 2), (s3y1, 1),
        (s2z, 3), (s2y1, 2), (s3y0, 1), (s2y0, 2), (s4, 0), (s5, 0), (s2y0, 3), (s2y1, 3), (s4, 1), (s5, 1),
        (s6, 0), (s3y1, 2), (s3y0, 2), (s3z, 2), (s6, 1), (s1a, 4), (s1a, 5), (s3z, 3), (s7, 0), (s3y1, 3),
        (s1b, 4), (s3y0, 3), (s4, 2), (s2y0, 4), (s2y1, 4), (s7, 1), (s2z, 4), (s1b, 5), (s2z, 5), (s2y1, 5),
        (s8, 0), (s2y0, 5), (s5, 2), (s4, 3), (s8, 1), (s3z, 4), (s3y0, 4), (s3y1, 4), (s3y1, 5), (s3y0, 5),
        (s5, 3), (s3z, 5), (s6, 2), (s4, 4), (s4, 5), (s6, 3), (s5, 4), (s7, 2), (s6, 5), (s7, 3), (s6, 4),
        (s7, 4), (s8, 2), (s7, 5), (s9, 1), (s9, 0), (s8, 3), (s8, 4), (s9, 2), (s9, 5), (s9, 3), (s9, 4),
    )
    for stage, k in order:
        stage(k)
    links.drain()


def step(tokens, targets, global_params, drift, first_moment, second_moment, outer_momentum):
    in_hbm = pl.BlockSpec(memory_space=pltpu.HBM)
    in_vmem = pl.BlockSpec(memory_space=pltpu.VMEM)
    p1, p2 = PROWS
    return pl.pallas_call(
        kernel,
        out_shape=(jax.ShapeDtypeStruct((ROWS, KV), F32),) * 2,
        in_specs=[in_hbm] * 7,
        out_specs=(in_vmem, in_vmem),
        scratch_shapes=[
            pltpu.VMEM((TOK, D), BF16),
            pltpu.VMEM((D, TOK), BF16),
            pltpu.VMEM((NS, 2, ROWS, H), BF16),
            pltpu.VMEM((TOK, KV), BF16),
            pltpu.VMEM((ROWS, KV), F32),
            pltpu.VMEM((ROWS, KV), F32),
            pltpu.VMEM((ROWS, KV), F32),
            pltpu.VMEM((ROWS, KV), F32),
            pltpu.VMEM((ROWS, KV), F32),
            pltpu.VMEM((2, 2, p1, H), BF16),
            pltpu.VMEM((2, 2, 2, p1, H), BF16),
            pltpu.VMEM((2, p2, H), BF16),
            pltpu.VMEM((2, 2, p2, H), BF16),
            pltpu.VMEM((4, 2, p2, H), BF16),
            pltpu.VMEM((2, p1, H), BF16),
            pltpu.VMEM((2, ROWS, H), F32),
            pltpu.VMEM((ROWS, H), F32),
            pltpu.VMEM((3, ROWS // 4, H), F32),
            pltpu.VMEM((ROWS // 4, H), F32),
            pltpu.VMEM((8, sum(SIZE[N - FAST :]) // 4, H), F32),
            pltpu.VMEM((2, ROWS, H), F32),
            pltpu.SemaphoreType.DMA((5,)),
            pltpu.SemaphoreType.DMA((2, C)),
            pltpu.SemaphoreType.DMA((N_MESSAGES,)),
            pltpu.SemaphoreType.DMA((N_MESSAGES,)),
        ],
        compiler_params=pltpu.CompilerParams(
            collective_id=0, has_side_effects=True, vmem_limit_bytes=VMEM_KIB * 2**10
        ),
        cost_estimate=pl.CostEstimate(
            flops=4 * TOK * D * KV, bytes_accessed=24 * 2**20, transcendentals=ROWS * KV
        ),
        name="inner_and_outer_step",
    )(tokens, targets, global_params, drift, first_moment, second_moment, outer_momentum)


def solution(mesh):
    in_specs = (
        P("replica", "fsdp", None),
        P("replica", "fsdp", None),
        P("fsdp", None),
        P("replica", "fsdp", None),
        P("replica", "fsdp", None),
        P("replica", "fsdp", None),
        P("fsdp", None),
    )
    out_specs = (P("fsdp", None), P("fsdp", None))
    return jax.shard_map(step, mesh=mesh, in_specs=in_specs, out_specs=out_specs, check_vma=False)
```

time: 153 us -> 146 us (0.954)
  other arithmetic: 5.65 us -> 0 us
  Pallas kernels: 146 us -> 141 us
  local copies, waits for them, and re-layouts: 0 us -> 3.67 us
    sub x1 -> x0, other arithmetic: 5.65 us -> none  [shards(): global_next = global_params - 0.7 * (0.9 * momentum_next + average)]
    pallas_call x1, Pallas kernels: 146 us -> 141 us  [step(): pl.pallas_call(kernel, out_shape=(jax.ShapeDtypeStruct((ROWS, KV), F32),)...]
    unnamed x0 -> x4, local copies, waits for them, and re-layouts: none -> 3.67 us
where the time goes in v2:
time: 146 us; the launch traced here: 145 us
  Pallas kernels  141 us (97%)
  local copies, waits for them, and re-layouts  3.67 us (3%)
    pallas_call x1, Pallas kernels, step(): pl.pallas_call(kernel, out_shape=(jax.ShapeDtypeStruct((ROWS, KV), F32),)...  141 us
    unnamed x4, local copies, waits for them, and re-layouts  3.67 us

profile of v2, /device:TPU:1, one launch (start us, length us, event | category | flops | bytes accessed | tf_op | source)
XLA Modules:
  0.0 145.4 jit_solution(7697545593254707509)
XLA Ops:
  0.6 0.0 copy-start
  0.6 1.0 copy-done
  1.7 141.1 %inner_and_outer_step.1 = (f32[1024,512]{1,0:T(8,128)S(1)}, f32[1024,512]{1,0:T(8,128)S(1)}) custom-call(bf16[1,512,8192]{2,1,0:T(8,128)(2,1)} %tok_hbm.1, bf16[1,512,512]{2,1,0:T(8,128)(2,1)S(1)} %copy-done, f32[1024,512]{1,0:T(8,128)} %gp_hbm.1, f32[1,1024,512]{2,1,0:T(8,128)} %dr_hbm.1, f32[1,1024,512]{2,1,0:T(8,128)} %m_hbm.1, f32[1,1024,512]{2,1,0:T(8,128)} %v_hbm.1, ...), custom_call_target="tpu_custom_call" | custom-call | flops 8589934592 | bytes 25165824 | tf_op jit(solution)/shard_map/inner_and_outer_step/pallas_call | solution.py:416
  142.7 1.3 copy.11
  144.1 1.3 copy.12
Async XLA Ops:
  0.6 1.0 copy-start

commit v3 on v2

--- a/solution.py
+++ b/solution.py
@@ -36,33 +36,25 @@
 class Links:
     def __init__(self, send_sems, recv_sems):
         self.send_sems, self.recv_sems = send_sems, recv_sems
-        self.index, self.sent = {}, []
-
-    def _sems(self, name):
-        i = self.index.setdefault(name, len(self.index))
-        return self.send_sems.at[i], self.recv_sems.at[i]
-
-    def send(self, name, src, dst, target):
-        s, r = self._sems(name)
-        copy = pltpu.make_async_remote_copy(
-            src_ref=src, dst_ref=dst, send_sem=s, recv_sem=r, device_id=target, device_id_type=MESH
-        )
-        copy.start()
-        self.sent.append(copy)
-
-    def recv(self, name, dst, anyone):
-        s, r = self._sems(name)
+        self.index = {}
+
+    def _sem(self, name):
+        return self.recv_sems.at[self.index.setdefault(name, len(self.index))]
+
+    def send(self, phase, name, src, dst, target):
         pltpu.make_async_remote_copy(
-            src_ref=dst, dst_ref=dst, send_sem=s, recv_sem=r, device_id=anyone, device_id_type=MESH
-        ).wait_recv()
-
-    def drain(self):
-        for copy in self.sent:
-            copy.wait_send()
-        self.sent = []
-
-
-N_MESSAGES = 208
+            src_ref=src, dst_ref=dst, send_sem=self.send_sems.at[phase], recv_sem=self._sem(name),
+            device_id=target, device_id_type=MESH,
+        ).start()
+
+    def recv(self, name, like):
+        pltpu.make_async_copy(like, like, self._sem(name)).wait()
+
+    def sent(self, phase, like):
+        pltpu.make_async_copy(like, like, self.send_sems.at[phase]).wait()
+
+
+N_MESSAGES = 10 * C + 14 * N - 2 * FAST
 
 
 def kernel(
@@ -126,7 +118,7 @@
         return w.at[s, :, rows] if h is None else w.at[s, h, rows]
 
     def wsend(name, piece, target):
-        links.send(name, piece, piece, target)
+        links.send(0, name, piece, piece, target)
 
     for k in range(C):
         if k:
@@ -153,31 +145,30 @@
         tokt[at, :] = tok[:, at].T
 
     for k in range(C):
-        links.recv(("za", k), wpiece(shard(y, oz), k), to_z)
+        links.recv(("za", k), wpiece(shard(y, oz), k))
         for h, target, _, _ in ydirs:
             wsend(("a2", h, k), wpiece(shard(y, oz), k, 0), target)
         for h, target, src, _ in ydirs:
-            links.recv(("a1", h, k), wpiece(shard(src, zl), k), target)
+            links.recv(("a1", h, k), wpiece(shard(src, zl), k))
             wsend(("a3", h, k), wpiece(shard(src, zl), k, None, h), target)
-            wsend(("z3", h, k), wpiece(shard(src, zl), k, 1), to_z)
+            wsend(("z3", k), wpiece(shard(src, zl), k, 1), to_z)
         dot_keys(shard(y, oz), k)
         dot_keys(shard(ym, zl), k)
         dot_keys(shard(yp, zl), k)
     for k in range(C):
         for h, target, src, _ in ydirs:
-            links.recv(("a3", h, k), wpiece(shard(y2, zl), k, None, h), target)
-            wsend(("z5", h, k), wpiece(shard(y2, zl), k, 1, h), to_z)
+            links.recv(("a3", h, k), wpiece(shard(y2, zl), k, None, h))
+            wsend(("z5", k), wpiece(shard(y2, zl), k, 1, h), to_z)
         for h, target, src, _ in ydirs:
-            links.recv(("a2", h, k), wpiece(shard(src, oz), k, 0), target)
-            wsend(("a4", h, k), wpiece(shard(src, oz), k, 0, h), target)
+            links.recv(("a2", h, k), wpiece(shard(src, oz), k, 0))
+            wsend(("a4", k), wpiece(shard(src, oz), k, 0, h), target)
         dot_keys(shard(y2, zl), k)
     for k in range(C):
-        for h, target, src, _ in ydirs:
-            links.recv(("z3", h, k), wpiece(shard(src, oz), k, 1), to_z)
-            dot_keys(shard(src, oz), k)
-        for h, target, src, _ in ydirs:
-            links.recv(("z5", h, k), wpiece(shard(y2, oz), k, 1, h), to_z)
-            links.recv(("a4", h, k), wpiece(shard(y2, oz), k, 0, h), target)
+        links.recv(("z3", k), w.at[pl.ds(0, 2), :, pl.ds(0, AP[1])])
+        dot_keys(shard(ym, oz), k)
+        dot_keys(shard(yp, oz), k)
+        links.recv(("z5", k), wpiece(shard(y2, oz), k, 1))
+        links.recv(("a4", k), wpiece(shard(y2, oz), k, 0))
         dot_keys(shard(y2, oz), k)
 
     load_tgt.wait()
@@ -185,7 +176,7 @@
         cols = pl.ds(h * H, H)
         tgt[:, cols] = (keys[h] - tgt[:, cols].astype(F32)).astype(BF16)
 
-    links.drain()
+    links.sent(0, w.at[pl.ds(0, NS - 1)])
     g = w
 
     def grads(s, k):
@@ -212,8 +203,8 @@
         for z in range(2):
             grads(shard(y2, z), k)
         for h, target, _, _ in ydirs:
-            links.send(("b1", h, k), gpair(y2, k, h), r_b1.at[h, :, part_rows(k, 0)], target)
-        links.send(("d1", 2, k), gpiece(shard(y2, oz), k, 1), r_d1.at[2, :, part_rows(k, 1)], to_z)
+            links.send(1, ("b1", h, k), gpair(y2, k, h), r_b1.at[h, :, part_rows(k, 0)], target)
+        links.send(1, ("da", k), gpiece(shard(y2, oz), k, 1), r_d1.at[3, :, part_rows(k, 1)], to_z)
 
     def s1b(k):
         @pl.loop(0, 2)
@@ -221,44 +212,46 @@
             for a in (yp, ym, y):
                 grads(shard(a, z), k)
 
-        for j, a in ((1, yp), (3, ym), (0, y)):
-            links.send(("d1", j, k), gpiece(shard(a, oz), k, 1), r_d1.at[j, :, part_rows(k, 1)], to_z)
+        for j, a in ((0, yp), (1, ym), (2, y)):
+            links.send(1, ("db", k), gpiece(shard(a, oz), k, 1), r_d1.at[j, :, part_rows(k, 1)], to_z)
 
     def s2y(h, k):
         p = part_rows(k, 0)
         _, target, _, dst = ydirs[h]
-        links.recv(("b1", h, k), r_b1.at[h, :, p], target)
+        links.recv(("b1", h, k), r_b1.at[h, :, p])
         own = gpair(dst, k, h)
         own[...] += r_b1[h, :, p]
-        links.send(("b2", h, k), gpair(dst, k), r_b2.at[h, :, :, p], target)
+        links.send(1, ("b2", k), gpair(dst, k), r_b2.at[h, :, :, p], target)
 
     def s2z(k):
         p = part_rows(k, 1)
-        links.recv(("d1", 2, k), r_d1.at[2, :, p], to_z)
+        links.recv(("da", k), r_d1.at[3, :, p])
         own = gpiece(shard(y2, zl), k, 1)
-        own[...] += r_d1[2, :, p]
+        own[...] += r_d1[3, :, p]
         for h, target, _, _ in ydirs:
-            links.send(("b3", h, k), gpiece(shard(y2, zl), k, 1, h), r_b3.at[h, p], target)
+            links.send(1, ("b3", h, k), gpiece(shard(y2, zl), k, 1, h), r_b3.at[h, p], target)
+
+    have_db = set()
 
     def s3y(h, k):
         p = part_rows(k, 1)
         _, target, _, dst = ydirs[h]
-        j = 1 if h == 0 else 3
-        links.recv(("d1", j, k), r_d1.at[j, :, p], to_z)
-        links.recv(("b3", h, k), r_b3.at[h, p], target)
+        if k not in have_db:
+            have_db.add(k)
+            links.recv(("db", k), r_d1.at[pl.ds(0, 3), :, p])
+        links.recv(("b3", h, k), r_b3.at[h, p])
         one = gpiece(shard(dst, zl), k, 1, h)
-        one[...] += r_d1[j, h, p] + r_b3[h, p]
+        one[...] += r_d1[h, h, p] + r_b3[h, p]
         two = gpiece(shard(dst, zl), k, 1, 1 - h)
-        two[...] += r_d1[j, 1 - h, p]
-        links.send(("b4", h, k), gpiece(shard(dst, zl), k, 1), r_b4.at[h, :, p], target)
+        two[...] += r_d1[h, 1 - h, p]
+        links.send(1, ("b4", k), gpiece(shard(dst, zl), k, 1), r_b4.at[h, :, p], target)
 
     def s3z(k):
         p = part_rows(k, 0)
-        for h, target, _, _ in ydirs:
-            links.recv(("b2", h, k), r_b2.at[h, :, :, p], target)
+        links.recv(("b2", k), r_b2.at[:, :, :, p])
         own = gpiece(shard(y, oz), k, 0)
         own[...] += r_b2[0, oz, :, p] + r_b2[1, oz, :, p]
-        links.send(("d2", k), own, r_d2.at[:, p], to_z)
+        links.send(1, ("d2", k), own, r_d2.at[:, p], to_z)
 
     def update(rows, cols, grad_sum):
         grad = grad_sum * (1.0 / (TOK * NS))
@@ -284,28 +277,26 @@
         if k == 0:
             load_m.wait()
             load_v.wait()
-        links.recv(("d2", k), r_d2.at[:, part_rows(k, 0)], to_z)
+        links.recv(("d2", k), r_d2.at[:, part_rows(k, 0)])
         updates(
             k, 0,
             lambda h, rows, p: (g[me, h, rows].astype(F32) + r_d2[h, p].astype(F32))
             + (r_b2[0, zl, h, p].astype(F32) + r_b2[1, zl, h, p].astype(F32)),
         )
-        links.recv(("d1", 0, k), r_d1.at[0, :, part_rows(k, 1)], to_z)
-        for h, target, _, _ in ydirs:
-            links.recv(("b4", h, k), r_b4.at[h, :, part_rows(k, 1)], target)
+        links.recv(("b4", k), r_b4.at[:, :, part_rows(k, 1)])
         updates(
             k, 1,
-            lambda h, rows, p: (g[me, h, rows].astype(F32) + r_d1[0, h, p].astype(F32))
+            lambda h, rows, p: (g[me, h, rows].astype(F32) + r_d1[2, h, p].astype(F32))
             + (r_b4[0, h, p].astype(F32) + r_b4[1, h, p].astype(F32)),
         )
         if k < N - FAST:
             rows = pl.ds(START[k], SIZE[k])
-            links.send(("c", k), delta.at[1 - c, rows], r_c.at[rows], to_xc[0])
+            links.send(2, ("c", k), delta.at[1 - c, rows], r_c.at[rows], to_xc[0])
         else:
             for j, other, target in others():
                 half = 1 - c if other else c
                 links.send(
-                    ("x", j, other, k), delta.at[half, x_rows(k, (x + j) % 4)], f_slot(j, other, k), target
+                    2, ("x", k), delta.at[half, x_rows(k, (x + j) % 4)], f_slot(j, other, k), target
                 )
 
     def others():
@@ -323,41 +314,43 @@
         q = SIZE[k] // 4
         return r_f.at[j * 2 + other, pl.ds((START[k] - START[N - FAST]) // 4, q)]
 
+    def f_slots(k):
+        q = SIZE[k] // 4
+        return r_f.at[pl.ds(1, 7), pl.ds((START[k] - START[N - FAST]) // 4, q)]
+
     def s5(k):
         rows = pl.ds(START[k], SIZE[k])
-        links.recv(("c", k), r_c.at[rows], to_xc[0])
+        links.recv(("c", k), r_c.at[rows])
         delta[c, rows] += r_c[rows]
         for j in (2, 1, 3):
             links.send(
-                ("x", j, k), delta.at[c, x_rows(k, (x + j) % 4)], r_x.at[j - 1, q_rows(k)], to_x[j]
+                2, ("x", k), delta.at[c, x_rows(k, (x + j) % 4)], r_x.at[j - 1, q_rows(k)], to_x[j]
             )
 
     def s6(k):
         at = x_rows(k, x)
         if k < N - FAST:
             p = q_rows(k)
-            for j in (1, 3, 2):
-                links.recv(("x", j, k), r_x.at[j - 1, p], to_x[j])
+            links.recv(("x", k), r_x.at[:, p])
             delta[c, at] += r_x[0, p] + r_x[1, p] + r_x[2, p]
         else:
-            for j, other, target in reversed(others()):
-                links.recv(("x", j, other, k), f_slot(j, other, k), target)
+            links.recv(("x", k), f_slots(k))
             total = delta[c, at]
             for j, other, _ in others():
                 total += f_slot(j, other, k)[...]
             delta[c, at] = total
-        links.send(("zh", k), delta.at[c, at], r_z.at[q_rows(k)], to_zh)
+        links.send(2, ("zh", k), delta.at[c, at], r_z.at[q_rows(k)], to_zh)
 
     def s7(k):
-        links.recv(("zh", k), r_z.at[q_rows(k)], to_zh)
+        links.recv(("zh", k), r_z.at[q_rows(k)])
         at = x_rows(k, x)
         avg[c, at] = (delta[c, at] + r_z[q_rows(k)]) * (1.0 / REPLICAS)
         if k < N - FAST:
             for j in (2, 1, 3):
-                links.send(("xg", j, k), avg.at[c, at], avg.at[c, at], to_x[j])
+                links.send(2, ("xg", k), avg.at[c, at], avg.at[c, at], to_x[j])
         else:
             for j, other, target in others():
-                links.send(("xg", j, other, k), avg.at[c, at], avg.at[c, at], target)
+                links.send(2, ("xg", k), avg.at[c, at], avg.at[c, at], target)
 
     def outer(k, half):
         sub = 32
@@ -372,10 +365,9 @@
             new_global[rows, cols] = gp[rows, cols] - 0.7 * (0.9 * momentum_next + average)
 
     def s8(k):
-        for j in (1, 3, 2):
-            links.recv(("xg", j, k), avg.at[c, x_rows(k, (x + 4 - j) % 4)], to_x[j])
+        links.recv(("xg", k), r_x.at[:, q_rows(k)])
         rows = pl.ds(START[k], SIZE[k])
-        links.send(("cg", k), avg.at[c, rows], avg.at[c, rows], to_xc[0])
+        links.send(2, ("cg", k), avg.at[c, rows], avg.at[c, rows], to_xc[0])
         if k == 0:
             load_om.wait()
         outer(k, c)
@@ -383,30 +375,30 @@
     def s9(k):
         if k < N - FAST:
             rows = pl.ds(START[k], SIZE[k])
-            links.recv(("cg", k), avg.at[1 - c, rows], to_xc[0])
+            links.recv(("cg", k), avg.at[1 - c, rows])
             outer(k, 1 - c)
         else:
-            for j, other, target in reversed(others()):
-                half = 1 - c if other else c
-                links.recv(("xg", j, other, k), avg.at[half, x_rows(k, (x + 4 - j) % 4)], target)
+            links.recv(("xg", k), f_slots(k))
             outer(k, 0)
             outer(k, 1)
 
     s2y0, s2y1 = functools.partial(s2y, 0), functools.partial(s2y, 1)
     s3y0, s3y1 = functools.partial(s3y, 0), functools.partial(s3y, 1)
     order = (
-        (s1a, 3), (s1a, 0), (s1b, 0), (s1a, 1), (s2y1, 0), (s2y0, 0), (s1b, 1), (s2y1, 1), (s2y0, 1), (s2z, 0),
-        (s2z, 1), (s1a, 2), (s3z, 0), (s3y1, 0), (s3y0, 0), (s1b, 3), (s2z, 2), (s3z, 1), (s1b, 2), (s3y1, 1),
-        (s2z, 3), (s2y1, 2), (s3y0, 1), (s2y0, 2), (s4, 0), (s5, 0), (s2y0, 3), (s2y1, 3), (s4, 1), (s5, 1),
-        (s6, 0), (s3y1, 2), (s3y0, 2), (s3z, 2), (s6, 1), (s1a, 4), (s1a, 5), (s3z, 3), (s7, 0), (s3y1, 3),
-        (s1b, 4), (s3y0, 3), (s4, 2), (s2y0, 4), (s2y1, 4), (s7, 1), (s2z, 4), (s1b, 5), (s2z, 5), (s2y1, 5),
-        (s8, 0), (s2y0, 5), (s5, 2), (s4, 3), (s8, 1), (s3z, 4), (s3y0, 4), (s3y1, 4), (s3y1, 5), (s3y0, 5),
-        (s5, 3), (s3z, 5), (s6, 2), (s4, 4), (s4, 5), (s6, 3), (s5, 4), (s7, 2), (s6, 5), (s7, 3), (s6, 4),
-        (s7, 4), (s8, 2), (s7, 5), (s9, 1), (s9, 0), (s8, 3), (s8, 4), (s9, 2), (s9, 5), (s9, 3), (s9, 4),
+        (s1a, 3), (s1a, 0), (s1b, 0), (s1a, 1), (s1b, 1), (s2z, 0), (s1a, 2), (s2y1, 0), (s2y0, 0), (s3y1, 0),
+        (s2z, 1), (s2y1, 1), (s3y0, 0), (s2y0, 1), (s3z, 0), (s3y0, 1), (s1b, 2), (s3y1, 1), (s2y1, 2),
+        (s2y0, 2), (s2z, 3), (s4, 0), (s5, 0), (s3z, 1), (s1b, 3), (s2z, 2), (s2y1, 3), (s2y0, 3), (s6, 0),
+        (s1a, 4), (s3z, 2), (s4, 1), (s3y0, 2), (s3y1, 2), (s5, 1), (s1a, 5), (s3y0, 3), (s3z, 3), (s3y1, 3),
+        (s1b, 4), (s1b, 5), (s2y0, 4), (s2y1, 4), (s2z, 4), (s7, 0), (s4, 2), (s2z, 5), (s6, 1), (s2y0, 5),
+        (s2y1, 5), (s4, 3), (s5, 2), (s3z, 4), (s3y0, 4), (s3y1, 4), (s5, 3), (s3y1, 5), (s8, 0), (s3z, 5),
+        (s7, 1), (s3y0, 5), (s4, 4), (s6, 2), (s5, 4), (s4, 5), (s6, 3), (s7, 2), (s6, 4), (s8, 1), (s6, 5),
+        (s7, 3), (s9, 0), (s7, 4), (s7, 5), (s8, 2), (s8, 3), (s9, 1), (s8, 4), (s9, 2), (s9, 3), (s9, 5),
+        (s9, 4),
     )
     for stage, k in order:
         stage(k)
-    links.drain()
+    links.sent(1, tokt.at[pl.ds(0, (NS - 1) * ROWS)])
+    links.sent(2, tokt.at[pl.ds(0, 15 * ROWS // 4)])
 
 
 def step(tokens, targets, global_params, drift, first_moment, second_moment, outer_momentum):
@@ -442,7 +434,7 @@
             pltpu.VMEM((2, ROWS, H), F32),
             pltpu.SemaphoreType.DMA((5,)),
             pltpu.SemaphoreType.DMA((2, C)),
-            pltpu.SemaphoreType.DMA((N_MESSAGES,)),
+            pltpu.SemaphoreType.DMA((3,)),
             pltpu.SemaphoreType.DMA((N_MESSAGES,)),
         ],
         compiler_params=pltpu.CompilerParams(

time: 146 us -> 139 us (0.952)
  Pallas kernels: 141 us -> 134 us
    pallas_call x1, Pallas kernels: 141 us -> 134 us  [step(): pl.pallas_call(kernel, out_shape=(jax.ShapeDtypeStruct((ROWS, KV), F32),)...]
where the time goes in v3:
time: 139 us
  Pallas kernels  134 us (96%)
  local copies, waits for them, and re-layouts  3.67 us (3%)
    pallas_call x1, Pallas kernels, step(): pl.pallas_call(kernel, out_shape=(jax.ShapeDtypeStruct((ROWS, KV), F32),)...  134 us
    unnamed x4, local copies, waits for them, and re-layouts  3.67 us

profile of v3, /device:TPU:1, one launch (start us, length us, event | category | flops | bytes accessed | tf_op | source)
XLA Modules:
  0.0 138.7 jit_solution(9703044517289199010)
XLA Ops:
  0.6 0.0 copy-start
  0.6 1.0 copy-done
  1.7 134.3 %inner_and_outer_step.1 = (f32[1024,512]{1,0:T(8,128)S(1)}, f32[1024,512]{1,0:T(8,128)S(1)}) custom-call(bf16[1,512,8192]{2,1,0:T(8,128)(2,1)} %tok_hbm.1, bf16[1,512,512]{2,1,0:T(8,128)(2,1)S(1)} %copy-done, f32[1024,512]{1,0:T(8,128)} %gp_hbm.1, f32[1,1024,512]{2,1,0:T(8,128)} %dr_hbm.1, f32[1,1024,512]{2,1,0:T(8,128)} %m_hbm.1, f32[1,1024,512]{2,1,0:T(8,128)} %v_hbm.1, ...), custom_call_target="tpu_custom_call" | custom-call | flops 8589934592 | bytes 25165824 | tf_op jit(solution)/shard_map/inner_and_outer_step/pallas_call | solution.py:408
  136.0 1.3 copy.11
  137.3 1.3 copy.12
Async XLA Ops:
  0.6 1.0 copy-start

commit v4 on v3

--- a/solution.py
+++ b/solution.py
@@ -401,7 +401,7 @@
     links.sent(2, tokt.at[pl.ds(0, 15 * ROWS // 4)])
 
 
-def step(tokens, targets, global_params, drift, first_moment, second_moment, outer_momentum):
+def step(*arrays):
     in_hbm = pl.BlockSpec(memory_space=pltpu.HBM)
     in_vmem = pl.BlockSpec(memory_space=pltpu.VMEM)
     p1, p2 = PROWS
@@ -444,7 +444,31 @@
             flops=4 * TOK * D * KV, bytes_accessed=24 * 2**20, transcendentals=ROWS * KV
         ),
         name="inner_and_outer_step",
-    )(tokens, targets, global_params, drift, first_moment, second_moment, outer_momentum)
+    )(*(pltpu.with_memory_space_constraint(a, pltpu.HBM) for a in arrays))
+
+
+def write_kernel(a_ref, b_ref, a_hbm, b_hbm, sems):
+    copies = []
+    for i, (src, dst) in enumerate(((a_ref, a_hbm), (b_ref, b_hbm))):
+        for q in range(2):
+            rows = pl.ds(q * ROWS // 2, ROWS // 2)
+            copies.append(pltpu.make_async_copy(src.at[rows], dst.at[rows], sems.at[i, q]))
+    for copy in copies:
+        copy.start()
+    for copy in copies:
+        copy.wait()
+
+
+def whole(*arrays):
+    return pl.pallas_call(
+        write_kernel,
+        out_shape=(jax.ShapeDtypeStruct((ROWS, KV), F32),) * 2,
+        in_specs=[pl.BlockSpec(memory_space=pl.ANY)] * 2,
+        out_specs=(pl.BlockSpec(memory_space=pltpu.HBM),) * 2,
+        scratch_shapes=[pltpu.SemaphoreType.DMA((2, 2))],
+        compiler_params=pltpu.CompilerParams(vmem_limit_bytes=2**20),
+        name="write_results",
+    )(*step(*arrays))
 
 
 def solution(mesh):
@@ -458,4 +482,4 @@
         P("fsdp", None),
     )
     out_specs = (P("fsdp", None), P("fsdp", None))
-    return jax.shard_map(step, mesh=mesh, in_specs=in_specs, out_specs=out_specs, check_vma=False)
+    return jax.shard_map(whole, mesh=mesh, in_specs=in_specs, out_specs=out_specs, check_vma=False)

time: 139 us -> 137 us (0.986)
  local copies, waits for them, and re-layouts: 3.67 us -> 0 us
  Pallas kernels: 134 us -> 136 us
    unnamed x4 -> x0, local copies, waits for them, and re-layouts: 3.67 us -> none
    pallas_call x0 -> x1, Pallas kernels: none -> 2.04 us  [whole(): pl.pallas_call(write_kernel, out_shape=(jax.ShapeDtypeStruct((ROWS, KV),...]
where the time goes in v4:
time: 137 us
  Pallas kernels  136 us (99%)
    pallas_call x1, Pallas kernels, step(): pl.pallas_call(kernel, out_shape=(jax.ShapeDtypeStruct((ROWS, KV), F32),)...  134 us

profile of v4, /device:TPU:1, one launch (start us, length us, event | category | flops | bytes accessed | tf_op | source)
XLA Modules:
  0.0 137.1 jit_solution(5770614917050578448)
XLA Ops:
  0.6 134.4 %inner_and_outer_step.1 = (f32[1024,512]{1,0:T(8,128)S(1)}, f32[1024,512]{1,0:T(8,128)S(1)}) custom-call(bf16[1,512,8192]{2,1,0:T(8,128)(2,1)} %tok_hbm.1, bf16[1,512,512]{2,1,0:T(8,128)(2,1)} %tgt_hbm.1, f32[1024,512]{1,0:T(8,128)} %gp_hbm.1, f32[1,1024,512]{2,1,0:T(8,128)} %dr_hbm.1, f32[1,1024,512]{2,1,0:T(8,128)} %m_hbm.1, f32[1,1024,512]{2,1,0:T(8,128)} %v_hbm.1, ...), custom_call_target="tpu_custom_call" | custom-call | flops 8589934592 | bytes 25165824 | tf_op jit(solution)/shard_map/inner_and_outer_step/pallas_call | solution.py:408
  135.1 2.0 %write_results.1 = (f32[1024,512]{1,0:T(8,128)}, f32[1024,512]{1,0:T(8,128)}) custom-call(f32[1024,512]{1,0:T(8,128)S(1)} %get-tuple-element.4.a_ref, f32[1024,512]{1,0:T(8,128)S(1)} %get-tuple-element.5.b_ref), custom_call_target="tpu_custom_call" | custom-call | tf_op jit(solution)/shard_map/write_results/pallas_call | solution.py:463

commit v5 on v4

--- a/solution.py
+++ b/solution.py
@@ -22,13 +22,15 @@
 C = 4
 R = ROWS // C
 AP = (144, 112)
-GROUPS = ((144, 112), (160, 96), (144, 112), (64, 64), (48, 16), (32, 32))
+GROUPS = ((160, 96), (144, 112), (112, 80), (112, 80), (32, 32), (32, 32))
 N = len(GROUPS)
 FAST = 1
 SIZE = [sum(p) for p in GROUPS]
 START = [sum(SIZE[:k]) for k in range(N)]
 PSTART = [[sum(p[i] for p in GROUPS[:k]) for k in range(N)] for i in range(2)]
 PROWS = [sum(p[i] for p in GROUPS) for i in range(2)]
+WIDE = 2
+LATE = START[WIDE]
 REPLICAS = 16
 VMEM_KIB = 50176
 
@@ -54,13 +56,17 @@
         pltpu.make_async_copy(like, like, self.send_sems.at[phase]).wait()
 
 
+AVERAGE_KIB = sum(
+    SIZE[k] * (15 if k < WIDE else 10 if k < N - FAST else 8) // 4 for k in range(N)
+)
 N_MESSAGES = 10 * C + 14 * N - 2 * FAST
 
 
 def kernel(
     tok_hbm, tgt_hbm, gp_hbm, dr_hbm, m_hbm, v_hbm, om_hbm, new_global, new_momentum,
     tok, tokt, w, tgt, gp, dr, mo, ve, om,
-    r_b1, r_b2, r_b3, r_b4, r_d1, r_d2, delta, r_c, r_x, r_z, r_f, avg,
+    r_b1, r_b2, r_b3, r_b4, r_d1, r_d2, delta, r_c, r_x, r_z, avg,
+    late_sum, late_x, late_f, late_avg,
     load_sem, part_sem, send_sems, recv_sems,
 ):
     rep = lax.axis_index("replica")
@@ -293,10 +299,12 @@
             rows = pl.ds(START[k], SIZE[k])
             links.send(2, ("c", k), delta.at[1 - c, rows], r_c.at[rows], to_xc[0])
         else:
+            rows = pl.ds(START[k], SIZE[k])
+            late_sum[:, pl.ds(START[k] - LATE, SIZE[k])] = delta[:, rows].astype(BF16)
             for j, other, target in others():
                 half = 1 - c if other else c
                 links.send(
-                    2, ("x", k), delta.at[half, x_rows(k, (x + j) % 4)], f_slot(j, other, k), target
+                    2, ("x", k), late_sum.at[half, late_rows(k, (x + j) % 4)], f_slot(j, other, k), target
                 )
 
     def others():
@@ -307,75 +315,96 @@
         q = SIZE[k] // 4
         return pl.ds(pl.multiple_of(START[k] + a * q, 8), q)
 
+    def late_rows(k, a):
+        q = SIZE[k] // 4
+        return pl.ds(pl.multiple_of(START[k] - LATE + a * q, 16), q)
+
     def q_rows(k):
         return pl.ds(START[k] // 4, SIZE[k] // 4)
 
+    def x_slots(k):
+        if k < WIDE:
+            return r_x.at[:, q_rows(k)]
+        return late_x.at[:, pl.ds((START[k] - LATE) // 4, SIZE[k] // 4)]
+
     def f_slot(j, other, k):
         q = SIZE[k] // 4
-        return r_f.at[j * 2 + other, pl.ds((START[k] - START[N - FAST]) // 4, q)]
+        return late_f.at[j * 2 + other, pl.ds((START[k] - START[N - FAST]) // 4, q)]
 
     def f_slots(k):
         q = SIZE[k] // 4
-        return r_f.at[pl.ds(1, 7), pl.ds((START[k] - START[N - FAST]) // 4, q)]
+        return late_f.at[pl.ds(1, 7), pl.ds((START[k] - START[N - FAST]) // 4, q)]
 
     def s5(k):
         rows = pl.ds(START[k], SIZE[k])
         links.recv(("c", k), r_c.at[rows])
         delta[c, rows] += r_c[rows]
+        if k >= WIDE:
+            late_sum[c, pl.ds(START[k] - LATE, SIZE[k])] = delta[c, rows].astype(BF16)
         for j in (2, 1, 3):
-            links.send(
-                2, ("x", k), delta.at[c, x_rows(k, (x + j) % 4)], r_x.at[j - 1, q_rows(k)], to_x[j]
-            )
+            at = (x + j) % 4
+            piece = delta.at[c, x_rows(k, at)] if k < WIDE else late_sum.at[c, late_rows(k, at)]
+            links.send(2, ("x", k), piece, x_slots(k).at[j - 1], to_x[j])
 
     def s6(k):
         at = x_rows(k, x)
         if k < N - FAST:
-            p = q_rows(k)
-            links.recv(("x", k), r_x.at[:, p])
-            delta[c, at] += r_x[0, p] + r_x[1, p] + r_x[2, p]
+            got = x_slots(k)
+            links.recv(("x", k), got)
+            delta[c, at] += got[0].astype(F32) + got[1].astype(F32) + got[2].astype(F32)
         else:
             links.recv(("x", k), f_slots(k))
             total = delta[c, at]
             for j, other, _ in others():
-                total += f_slot(j, other, k)[...]
+                total += f_slot(j, other, k)[...].astype(F32)
             delta[c, at] = total
         links.send(2, ("zh", k), delta.at[c, at], r_z.at[q_rows(k)], to_zh)
 
     def s7(k):
         links.recv(("zh", k), r_z.at[q_rows(k)])
         at = x_rows(k, x)
-        avg[c, at] = (delta[c, at] + r_z[q_rows(k)]) * (1.0 / REPLICAS)
+        average = (delta[c, at] + r_z[q_rows(k)]) * (1.0 / REPLICAS)
+        if k < WIDE:
+            piece = avg.at[c, at]
+            piece[...] = average
+        else:
+            piece = late_avg.at[c, late_rows(k, x)]
+            piece[...] = average.astype(BF16)
         if k < N - FAST:
             for j in (2, 1, 3):
-                links.send(2, ("xg", k), avg.at[c, at], avg.at[c, at], to_x[j])
+                links.send(2, ("xg", k), piece, piece, to_x[j])
         else:
             for j, other, target in others():
-                links.send(2, ("xg", k), avg.at[c, at], avg.at[c, at], target)
+                links.send(2, ("xg", k), piece, piece, target)
+
+    def averages(half, k):
+        if k < WIDE:
+            return avg.at[half, pl.ds(START[k], SIZE[k])]
+        return late_avg.at[half, pl.ds(START[k] - LATE, SIZE[k])]
 
     def outer(k, half):
         sub = 32
 
         @pl.loop(0, SIZE[k] // sub)
         def _(i):
-            rows = pl.ds(START[k] + pl.multiple_of(i * sub, sub), sub)
+            off = pl.multiple_of(i * sub, sub)
+            rows = pl.ds(START[k] + off, sub)
             cols = pl.ds(pl.multiple_of(half * H, H), H)
-            average = avg[half, rows]
+            average = averages(half, k)[pl.ds(off, sub)].astype(F32)
             momentum_next = 0.9 * om[rows, cols] + average
             new_momentum[rows, cols] = momentum_next
             new_global[rows, cols] = gp[rows, cols] - 0.7 * (0.9 * momentum_next + average)
 
     def s8(k):
-        links.recv(("xg", k), r_x.at[:, q_rows(k)])
-        rows = pl.ds(START[k], SIZE[k])
-        links.send(2, ("cg", k), avg.at[c, rows], avg.at[c, rows], to_xc[0])
+        links.recv(("xg", k), x_slots(k))
+        links.send(2, ("cg", k), averages(c, k), averages(c, k), to_xc[0])
         if k == 0:
             load_om.wait()
         outer(k, c)
 
     def s9(k):
         if k < N - FAST:
-            rows = pl.ds(START[k], SIZE[k])
-            links.recv(("cg", k), avg.at[1 - c, rows])
+            links.recv(("cg", k), averages(1 - c, k))
             outer(k, 1 - c)
         else:
             links.recv(("xg", k), f_slots(k))
@@ -385,20 +414,20 @@
     s2y0, s2y1 = functools.partial(s2y, 0), functools.partial(s2y, 1)
     s3y0, s3y1 = functools.partial(s3y, 0), functools.partial(s3y, 1)
     order = (
-        (s1a, 3), (s1a, 0), (s1b, 0), (s1a, 1), (s1b, 1), (s2z, 0), (s1a, 2), (s2y1, 0), (s2y0, 0), (s3y1, 0),
-        (s2z, 1), (s2y1, 1), (s3y0, 0), (s2y0, 1), (s3z, 0), (s3y0, 1), (s1b, 2), (s3y1, 1), (s2y1, 2),
-        (s2y0, 2), (s2z, 3), (s4, 0), (s5, 0), (s3z, 1), (s1b, 3), (s2z, 2), (s2y1, 3), (s2y0, 3), (s6, 0),
-        (s1a, 4), (s3z, 2), (s4, 1), (s3y0, 2), (s3y1, 2), (s5, 1), (s1a, 5), (s3y0, 3), (s3z, 3), (s3y1, 3),
-        (s1b, 4), (s1b, 5), (s2y0, 4), (s2y1, 4), (s2z, 4), (s7, 0), (s4, 2), (s2z, 5), (s6, 1), (s2y0, 5),
-        (s2y1, 5), (s4, 3), (s5, 2), (s3z, 4), (s3y0, 4), (s3y1, 4), (s5, 3), (s3y1, 5), (s8, 0), (s3z, 5),
-        (s7, 1), (s3y0, 5), (s4, 4), (s6, 2), (s5, 4), (s4, 5), (s6, 3), (s7, 2), (s6, 4), (s8, 1), (s6, 5),
-        (s7, 3), (s9, 0), (s7, 4), (s7, 5), (s8, 2), (s8, 3), (s9, 1), (s8, 4), (s9, 2), (s9, 3), (s9, 5),
+        (s1a, 4), (s1a, 0), (s1b, 0), (s1a, 2), (s2z, 0), (s1a, 1), (s1a, 3), (s2y1, 0), (s2y0, 0), (s1b, 1),
+        (s2y0, 1), (s1b, 2), (s2y1, 1), (s3z, 0), (s2z, 1), (s3y1, 0), (s2y1, 2), (s3y0, 0), (s3z, 1),
+        (s2y0, 2), (s3y0, 1), (s1b, 4), (s1b, 3), (s2y0, 3), (s3y1, 1), (s4, 0), (s2z, 2), (s2y1, 3), (s5, 0),
+        (s3z, 2), (s4, 1), (s2z, 3), (s1a, 5), (s3y1, 2), (s2y0, 4), (s6, 0), (s3y0, 2), (s2y1, 4), (s3z, 3),
+        (s5, 1), (s2z, 4), (s3y1, 3), (s3y0, 3), (s2z, 5), (s1b, 5), (s2y0, 5), (s7, 0), (s2y1, 5), (s4, 2),
+        (s3y0, 4), (s3z, 4), (s3y1, 4), (s6, 1), (s4, 3), (s5, 2), (s3y1, 5), (s3y0, 5), (s3z, 5), (s4, 4),
+        (s5, 3), (s5, 4), (s6, 2), (s4, 5), (s8, 0), (s7, 1), (s6, 3), (s6, 4), (s6, 5), (s7, 2), (s7, 3),
+        (s8, 1), (s7, 4), (s7, 5), (s9, 0), (s8, 2), (s9, 1), (s8, 3), (s8, 4), (s9, 2), (s9, 5), (s9, 3),
         (s9, 4),
     )
     for stage, k in order:
         stage(k)
     links.sent(1, tokt.at[pl.ds(0, (NS - 1) * ROWS)])
-    links.sent(2, tokt.at[pl.ds(0, 15 * ROWS // 4)])
+    links.sent(2, tokt.at[pl.ds(0, AVERAGE_KIB)])
 
 
 def step(*arrays):
@@ -428,10 +457,13 @@
             pltpu.VMEM((2, p1, H), BF16),
             pltpu.VMEM((2, ROWS, H), F32),
             pltpu.VMEM((ROWS, H), F32),
-            pltpu.VMEM((3, ROWS // 4, H), F32),
+            pltpu.VMEM((3, LATE // 4, H), F32),
             pltpu.VMEM((ROWS // 4, H), F32),
-            pltpu.VMEM((8, sum(SIZE[N - FAST :]) // 4, H), F32),
-            pltpu.VMEM((2, ROWS, H), F32),
+            pltpu.VMEM((2, LATE, H), F32),
+            pltpu.VMEM((2, ROWS - LATE, H), BF16),
+            pltpu.VMEM((3, (ROWS - LATE) // 4, H), BF16),
+            pltpu.VMEM((8, sum(SIZE[N - FAST :]) // 4, H), BF16),
+            pltpu.VMEM((2, ROWS - LATE, H), BF16),
             pltpu.SemaphoreType.DMA((5,)),
             pltpu.SemaphoreType.DMA((2, C)),
             pltpu.SemaphoreType.DMA((3,)),

time: 137 us -> 136 us (level)
    pallas_call x1, Pallas kernels: 134 us -> 133 us  [step(): pl.pallas_call(kernel, out_shape=(jax.ShapeDtypeStruct((ROWS, KV), F32),)...]
where the time goes in v5:
time: 136 us; the launch traced here: 135 us
  Pallas kernels  135 us (99%)
    pallas_call x1, Pallas kernels, step(): pl.pallas_call(kernel, out_shape=(jax.ShapeDtypeStruct((ROWS, KV), F32),)...  133 us

profile of v5, /device:TPU:1, one launch (start us, length us, event | category | flops | bytes accessed | tf_op | source)
XLA Modules:
  0.0 135.4 jit_solution(5923193755890297628)
XLA Ops:
  0.6 132.8 %inner_and_outer_step.1 = (f32[1024,512]{1,0:T(8,128)S(1)}, f32[1024,512]{1,0:T(8,128)S(1)}) custom-call(bf16[1,512,8192]{2,1,0:T(8,128)(2,1)} %tok_hbm.1, bf16[1,512,512]{2,1,0:T(8,128)(2,1)} %tgt_hbm.1, f32[1024,512]{1,0:T(8,128)} %gp_hbm.1, f32[1,1024,512]{2,1,0:T(8,128)} %dr_hbm.1, f32[1,1024,512]{2,1,0:T(8,128)} %m_hbm.1, f32[1,1024,512]{2,1,0:T(8,128)} %v_hbm.1, ...), custom_call_target="tpu_custom_call" | custom-call | flops 8589934592 | bytes 25165824 | tf_op jit(solution)/shard_map/inner_and_outer_step/pallas_call | solution.py:437
  133.4 2.0 %write_results.1 = (f32[1024,512]{1,0:T(8,128)}, f32[1024,512]{1,0:T(8,128)}) custom-call(f32[1024,512]{1,0:T(8,128)S(1)} %get-tuple-element.4.a_ref, f32[1024,512]{1,0:T(8,128)S(1)} %get-tuple-element.5.b_ref), custom_call_target="tpu_custom_call" | custom-call | tf_op jit(solution)/shard_map/write_results/pallas_call | solution.py:495

commit v6 on v4

--- a/solution.py
+++ b/solution.py
@@ -22,7 +22,7 @@
 C = 4
 R = ROWS // C
 AP = (144, 112)
-GROUPS = ((144, 112), (160, 96), (144, 112), (64, 64), (48, 16), (32, 32))
+GROUPS = ((160, 96), (144, 112), (112, 80), (112, 80), (32, 32), (32, 32))
 N = len(GROUPS)
 FAST = 1
 SIZE = [sum(p) for p in GROUPS]
@@ -274,9 +274,6 @@
                 delta[h, rows] = update(rows, pl.ds(h * H, H), total(h, rows, p))
 
     def s4(k):
-        if k == 0:
-            load_m.wait()
-            load_v.wait()
         links.recv(("d2", k), r_d2.at[:, part_rows(k, 0)])
         updates(
             k, 0,
@@ -368,8 +365,6 @@
         links.recv(("xg", k), r_x.at[:, q_rows(k)])
         rows = pl.ds(START[k], SIZE[k])
         links.send(2, ("cg", k), avg.at[c, rows], avg.at[c, rows], to_xc[0])
-        if k == 0:
-            load_om.wait()
         outer(k, c)
 
     def s9(k):
@@ -385,16 +380,18 @@
     s2y0, s2y1 = functools.partial(s2y, 0), functools.partial(s2y, 1)
     s3y0, s3y1 = functools.partial(s3y, 0), functools.partial(s3y, 1)
     order = (
-        (s1a, 3), (s1a, 0), (s1b, 0), (s1a, 1), (s1b, 1), (s2z, 0), (s1a, 2), (s2y1, 0), (s2y0, 0), (s3y1, 0),
-        (s2z, 1), (s2y1, 1), (s3y0, 0), (s2y0, 1), (s3z, 0), (s3y0, 1), (s1b, 2), (s3y1, 1), (s2y1, 2),
-        (s2y0, 2), (s2z, 3), (s4, 0), (s5, 0), (s3z, 1), (s1b, 3), (s2z, 2), (s2y1, 3), (s2y0, 3), (s6, 0),
-        (s1a, 4), (s3z, 2), (s4, 1), (s3y0, 2), (s3y1, 2), (s5, 1), (s1a, 5), (s3y0, 3), (s3z, 3), (s3y1, 3),
-        (s1b, 4), (s1b, 5), (s2y0, 4), (s2y1, 4), (s2z, 4), (s7, 0), (s4, 2), (s2z, 5), (s6, 1), (s2y0, 5),
-        (s2y1, 5), (s4, 3), (s5, 2), (s3z, 4), (s3y0, 4), (s3y1, 4), (s5, 3), (s3y1, 5), (s8, 0), (s3z, 5),
-        (s7, 1), (s3y0, 5), (s4, 4), (s6, 2), (s5, 4), (s4, 5), (s6, 3), (s7, 2), (s6, 4), (s8, 1), (s6, 5),
-        (s7, 3), (s9, 0), (s7, 4), (s7, 5), (s8, 2), (s8, 3), (s9, 1), (s8, 4), (s9, 2), (s9, 3), (s9, 5),
-        (s9, 4),
+        (s1a, 4), (s1a, 2), (s1a, 1), (s1b, 1), (s1a, 3), (s1b, 3), (s1a, 0), (s2z, 1), (s2y1, 1), (s1b, 0),
+        (s2y0, 1), (s2y0, 0), (s2y1, 0), (s3z, 1), (s2z, 0), (s2z, 3), (s3y0, 1), (s3y1, 1), (s3z, 0),
+        (s2y0, 3), (s2y1, 3), (s3y1, 0), (s3y0, 0), (s1b, 2), (s2z, 2), (s2y0, 2), (s2y1, 2), (s4, 1), (s5, 1),
+        (s3y0, 3), (s3y1, 3), (s1b, 4), (s3z, 3), (s4, 0), (s2y1, 4), (s1a, 5), (s6, 1), (s2z, 4), (s5, 0),
+        (s2y0, 4), (s3y0, 2), (s3z, 2), (s1b, 5), (s3y1, 2), (s4, 3), (s2z, 5), (s2y0, 5), (s3y0, 4), (s7, 1),
+        (s2y1, 5), (s3y1, 4), (s3z, 4), (s6, 0), (s5, 3), (s4, 2), (s3y1, 5), (s3y0, 5), (s3z, 5), (s5, 2),
+        (s4, 4), (s5, 4), (s6, 3), (s4, 5), (s7, 0), (s8, 1), (s6, 2), (s7, 3), (s6, 4), (s6, 5), (s7, 2),
+        (s8, 0), (s7, 4), (s7, 5), (s8, 3), (s9, 1), (s8, 2), (s9, 0), (s8, 4), (s9, 3), (s9, 5), (s9, 4),
+        (s9, 2),
     )
+    for copy in (load_m, load_v, load_om):
+        copy.wait()
     for stage, k in order:
         stage(k)
     links.sent(1, tokt.at[pl.ds(0, (NS - 1) * ROWS)])

time: 137 us -> 137 us (level)
  no operation moved by 1% of the time
where the time goes in v6:
time: 137 us
  Pallas kernels  136 us (99%)
    pallas_call x1, Pallas kernels, step(): pl.pallas_call(kernel, out_shape=(jax.ShapeDtypeStruct((ROWS, KV), F32),)...  134 us

profile of v6, /device:TPU:1, one launch (start us, length us, event | category | flops | bytes accessed | tf_op | source)
XLA Modules:
  0.0 136.8 jit_solution(1614693662509719162)
XLA Ops:
  0.6 134.2 %inner_and_outer_step.1 = (f32[1024,512]{1,0:T(8,128)S(1)}, f32[1024,512]{1,0:T(8,128)S(1)}) custom-call(bf16[1,512,8192]{2,1,0:T(8,128)(2,1)} %tok_hbm.1, bf16[1,512,512]{2,1,0:T(8,128)(2,1)} %tgt_hbm.1, f32[1024,512]{1,0:T(8,128)} %gp_hbm.1, f32[1,1024,512]{2,1,0:T(8,128)} %dr_hbm.1, f32[1,1024,512]{2,1,0:T(8,128)} %m_hbm.1, f32[1,1024,512]{2,1,0:T(8,128)} %v_hbm.1, ...), custom_call_target="tpu_custom_call" | custom-call | flops 8589934592 | bytes 25165824 | tf_op jit(solution)/shard_map/inner_and_outer_step/pallas_call | solution.py:405
  134.8 2.0 %write_results.1 = (f32[1024,512]{1,0:T(8,128)}, f32[1024,512]{1,0:T(8,128)}) custom-call(f32[1024,512]{1,0:T(8,128)S(1)} %get-tuple-element.4.a_ref, f32[1024,512]{1,0:T(8,128)S(1)} %get-tuple-element.5.b_ref), custom_call_target="tpu_custom_call" | custom-call | tf_op jit(solution)/shard_map/write_results/pallas_call | solution.py:460

commit v7 on v5

--- a/solution.py
+++ b/solution.py
@@ -29,7 +29,7 @@
 START = [sum(SIZE[:k]) for k in range(N)]
 PSTART = [[sum(p[i] for p in GROUPS[:k]) for k in range(N)] for i in range(2)]
 PROWS = [sum(p[i] for p in GROUPS) for i in range(2)]
-WIDE = 2
+WIDE = 3
 LATE = START[WIDE]
 REPLICAS = 16
 VMEM_KIB = 50176

time: 136 us -> 136 us (level)
  no operation moved by 1% of the time
where the time goes in v7:
time: 136 us
  Pallas kernels  136 us (100%)
    pallas_call x1, Pallas kernels, step(): pl.pallas_call(kernel, out_shape=(jax.ShapeDtypeStruct((ROWS, KV), F32),)...  134 us

profile of v7, /device:TPU:1, one launch (start us, length us, event | category | flops | bytes accessed | tf_op | source)
XLA Modules:
  0.0 136.3 jit_solution(12393797438208804276)
XLA Ops:
  0.6 133.6 %inner_and_outer_step.1 = (f32[1024,512]{1,0:T(8,128)S(1)}, f32[1024,512]{1,0:T(8,128)S(1)}) custom-call(bf16[1,512,8192]{2,1,0:T(8,128)(2,1)} %tok_hbm.1, bf16[1,512,512]{2,1,0:T(8,128)(2,1)} %tgt_hbm.1, f32[1024,512]{1,0:T(8,128)} %gp_hbm.1, f32[1,1024,512]{2,1,0:T(8,128)} %dr_hbm.1, f32[1,1024,512]{2,1,0:T(8,128)} %m_hbm.1, f32[1,1024,512]{2,1,0:T(8,128)} %v_hbm.1, ...), custom_call_target="tpu_custom_call" | custom-call | flops 8589934592 | bytes 25165824 | tf_op jit(solution)/shard_map/inner_and_outer_step/pallas_call | solution.py:437
  134.3 2.0 %write_results.1 = (f32[1024,512]{1,0:T(8,128)}, f32[1024,512]{1,0:T(8,128)}) custom-call(f32[1024,512]{1,0:T(8,128)S(1)} %get-tuple-element.4.a_ref, f32[1024,512]{1,0:T(8,128)S(1)} %get-tuple-element.5.b_ref), custom_call_target="tpu_custom_call" | custom-call | tf_op jit(solution)/shard_map/write_results/pallas_call | solution.py:495
